TPU v7x, 32 devices: a whole 2x2x4 slice. The times are simulated.
32 devices in a mesh: grid: 8 (over y, x, core), band: 4 (over z).
Axes of the slice: x: 2, y: 2, z: 4, core: 2. Of those that a mesh axis runs over, the one named last changes fastest.
Arguments:
- residual: float32 [32, 64, 32, 384], P('band', 'grid')
- direction: float32 [32, 64, 32, 384], P('band', 'grid'), may hold values from -2 to 2
- solution: float32 [32, 64, 32, 384], P('band', 'grid'), may hold values from -6 to 6
- old_product: float32 [32], P('band'), may hold values from 157286.4 to 629145.6
- orbitals: bfloat16 [32, 64, 32, 384], P('band', 'grid')
- energies: float32 [32], replicated, may hold values from -3 to -0.3
- potential: float32 [64, 32, 384], P('grid'), may hold values from 0.5 to 3
- column_index: int32 [32], P('band'), may hold values from 0 to 95
- panel_index: int32 [32], P('band'), may hold values from 0 to 1
Outputs:
- new_solution: float32 [32, 64, 32, 384], P('band', 'grid')
- new_residual: float32 [32, 64, 32, 384], P('band', 'grid')
- new_direction: float32 [32, 64, 32, 384], P('band', 'grid')
- new_product: float32 [32], P('band')
All inputs are finite; a program needn't handle non-finite values.
Results may differ from a plain program's by a relative error of at most 0.00085.
Values may be sent and summed in bfloat16 or wider, within the bound.
No kernel may reach another device: no remote copies, remote signals or barrier semaphores. Data moves between devices by JAX's collectives and lax.ppermute only.
A program may use at most 128 MiB of HBM per device.

v0:
```python
import jax
import jax.numpy as jnp
from jax import lax
from jax.sharding import PartitionSpec as P

PB = 16


COEFFS = (-49.0 / 18.0, 3.0 / 2.0, -3.0 / 20.0, 1.0 / 90.0)


def extended(cells, sides, width):
    for axis, dim in sides:
        count = lax.axis_size(axis)
        ends = count - 1
        head = lax.slice_in_dim(cells, 0, width, axis=dim)
        tail = lax.slice_in_dim(cells, cells.shape[dim] - width, cells.shape[dim], axis=dim)
        cells = jnp.concatenate(
            [
                lax.ppermute(tail, axis, [(i, (i + 1) % count) for i in range(ends)]),
                cells,
                lax.ppermute(head, axis, [((i + 1) % count, i) for i in range(ends)]),
            ],
            axis=dim,
        )
    return cells


def stencil(padded, fields, shifted):
    extent_x, extent_y, extent_z = (fields.shape[1], fields.shape[2], fields.shape[3])
    widened = jnp.pad(padded, ((0, 0), (0, 0), (3, 3), (3, 3)))
    summed = 3.0 * COEFFS[0] * fields
    for offset in range(1, 4):
        beside_all = (
            widened[:, 3 + offset : 3 + offset + extent_x, 3 : 3 + extent_y, 3 : 3 + extent_z]
            + widened[:, 3 - offset : 3 - offset + extent_x, 3 : 3 + extent_y, 3 : 3 + extent_z]
        )
        beside_all = (
            beside_all
            + widened[:, 3 : 3 + extent_x, 3 + offset : 3 + offset + extent_y, 3 : 3 + extent_z]
            + widened[:, 3 : 3 + extent_x, 3 - offset : 3 - offset + extent_y, 3 : 3 + extent_z]
        )
        beside_all = (
            beside_all
            + widened[:, 3 : 3 + extent_x, 3 : 3 + extent_y, 3 + offset : 3 + offset + extent_z]
            + widened[:, 3 : 3 + extent_x, 3 : 3 + extent_y, 3 - offset : 3 - offset + extent_z]
        )
        summed = summed + COEFFS[offset] * beside_all
    return -0.5 * summed + shifted * fields


def cell_sum(left, right):
    return jnp.sum(left * right, axis=(1, 2, 3))


def on_device(
    residual,
    direction,
    solution,
    old_product,
    orbitals,
    energies,
    potential,
    column_index,
    panel_index,
):
    band_ids = lax.iota(jnp.int32, energies.shape[0])
    picked = jnp.where(
        band_ids[None, :] == (column_index // 3)[:, None], energies[None, :], jnp.float32(0.0)
    )
    energy = jnp.sum(picked, axis=1)
    shifted = potential[None] - energy[:, None, None, None]
    precond = shifted - 1.5 * COEFFS[0]
    start = residual / precond
    wave = lax.all_gather(orbitals, "band", axis=0, tiled=True)
    cells = float(residual.shape[1] * lax.axis_size("grid") * residual.shape[2] * residual.shape[3])
    member = band_ids[None, :] // PB == panel_index[:, None]
    correlation_local = jnp.einsum(
        "cxyz,bxyz->cb",
        start,
        wave,
        precision=lax.Precision.HIGHEST,
        preferred_element_type=jnp.float32,
    )
    correlation = lax.psum(correlation_local, "grid")
    chosen = jnp.where(member, correlation, jnp.float32(0.0)) / cells
    removed = jnp.einsum(
        "cb,bxyz->cxyz",
        chosen,
        wave,
        precision=lax.Precision.HIGHEST,
        preferred_element_type=jnp.float32,
    )
    projected, chosen = (start - removed, chosen)
    rr_now = lax.psum(cell_sum(residual, projected), "grid")
    new_dir = projected + (rr_now / old_product)[:, None, None, None] * direction
    padded = extended(new_dir.astype(jnp.bfloat16), (("grid", 1),), 3).astype(new_dir.dtype)
    image = stencil(padded, new_dir, shifted)
    curvature = lax.psum(cell_sum(new_dir, image), "grid")
    step_size = (rr_now / curvature)[:, None, None, None]
    return (solution + step_size * new_dir, residual - step_size * image, new_dir, rr_now)


def solution(mesh):
    return jax.shard_map(
        on_device,
        mesh=mesh,
        in_specs=(
            P("band", "grid", None, None),
            P("band", "grid", None, None),
            P("band", "grid", None, None),
            P("band"),
            P("band", "grid", None, None),
            P(),
            P("grid", None, None),
            P("band"),
            P("band"),
        ),
        out_specs=(
            P("band", "grid", None, None),
            P("band", "grid", None, None),
            P("band", "grid", None, None),
            P("band"),
        ),
        check_vma=False,
    )
```

profile of v0, /device:TPU:0, one launch (start us, length us, event | category | flops | bytes accessed | tf_op | source)
XLA Modules:
  0.0 232.9 jit_solution(18108845687687763765)
XLA Ops:
  7.2 0.0 copy-start
  7.2 0.0 all-gather.2.cloned.1.call-start
  7.3 3.6 %copy.14 = bf16[8,8,32,384]{3,0,2,1:T(8,128)(2,1)} copy(bf16[8,8,32,384]{3,2,1,0:T(8,128)(2,1)} %param.13) | data formatting | bytes 3145728 | tf_op args[4]
  10.9 0.0 all-gather.2.cloned.1.call-update
  10.9 0.5 and_select_fusion
  11.4 0.2 select_reduce_fusion
  11.6 117.5 %all-gather.2.cloned.1.call-done = bf16[32,8,32,384]{3,0,2,1:T(8,128)(2,1)} async-done(((bf16[8,8,32,384]{3,0,2,1:T(8,128)(2,1)}), bf16[32,8,32,384]{3,0,2,1:T(8,128)(2,1)}) %all-gather.2.cloned.1.call-update) | async-done | bytes 6291472 | tf_op jit(solution)/shard_map/all_gather | solution.py:75
  129.1 8.1 %convolution_bitcast_fusion = f32[8,32]{1,0:T(8,128)S(1)} fusion(bf16[32,8,32,384]{3,0,2,1:T(8,128)(2,1)} %all-gather.2.cloned.1.call-done, f32[8,8,32,384]{3,2,1,0:T(8,128)S(1)} %copy-done, f32[8]{0:T(128)S(1)} %select_reduce_fusion, f32[8,32,384]{2,1,0:T(8,128)S(1)} %copy-done.1), kind=kOutput, calls=%fused_computation.46 | convolution fusion | flops 304349184 | bytes 9831456 | tf_op jit(solution)/shard_map/cxyz,bxyz->cb/dot_general | solution.py:78
  137.2 13.8 %psum.21 = f32[8,32]{1,0:T(8,128)S(1)} all-reduce(f32[8,32]{1,0:T(8,128)S(1)} %convolution_bitcast_fusion), channel_id=1, replica_groups=mesh['grid'=8,'band'=4] {'grid'}, use_global_device_ids=true, to_apply=%region_1.2 | all-reduce | flops 256 | bytes 2048 | tf_op jit(solution)/shard_map/psum | solution.py:85
  151.1 0.0 copy-start.5
  151.1 7.8 %multiply_reduce_fusion.1 = (f32[8]{0:T(128)}, f32[8,8,32,384]{3,0,2,1:T(8,128)}) fusion(f32[8,8,32,384]{3,2,1,0:T(8,128)S(1)} %copy-done, bf16[32,8,32,384]{3,0,2,1:T(8,128)(2,1)} %all-gather.2.cloned.1.call-done, f32[8,32]{1,0:T(8,128)S(1)} %psum.21, s32[32]{0:T(128)} %and_select_fusion, s32[8]{0:T(128)S(1)} %copy-done.4, f32[8]{0:T(128)S(1)} %select_reduce_fusion, ...), kind=kOutput, calls=%fused_computation.43 | convolution fusion | flops 306709248 | bytes 12977376 | tf_op jit(solution)/shard_map/cb,bxyz->cxyz/dot_general | solution.py:87
  158.8 11.9 %psum.22 = f32[8]{0:T(128)S(1)} all-reduce(f32[8]{0:T(128)} %get-tuple-element.16), channel_id=1, replica_groups=mesh['grid'=8,'band'=4] {'grid'}, use_global_device_ids=true, to_apply=%region_3.4 | all-reduce | flops 8 | bytes 64 | tf_op jit(solution)/shard_map/psum | solution.py:95
  170.8 5.1 %fusion.34 = (bf16[8,8,32,384]{3,0,2,1:T(8,128)(2,1)S(1)}, f32[8,8,32,384]{3,0,2,1:T(8,128)S(1)}) fusion(f32[8,8,32,384]{3,0,2,1:T(8,128)} %get-tuple-element.17, f32[8,8,32,384]{3,2,1,0:T(8,128)} %param.10, f32[8]{0:T(128)S(1)} %div.35), kind=kLoop, calls=%fused_computation.64 | loop fusion | flops 2359296 | bytes 11010080 | tf_op jit(solution)/shard_map/convert_element_type | solution.py:97
  175.9 0.1 fusion.36
  176.0 1.8 collective-permute-start
  177.8 1.3 collective-permute-start.1
  179.1 2.2 copy.21
  181.3 0.4 collective-permute-done.1
  181.7 0.4 maximum_convert_fusion
  182.1 6.7 %multiply_reduce_fusion = (f32[8]{0:T(128)S(1)}, f32[8,8,32,384]{3,0,2,1:T(8,128)}) fusion(f32[8,8,32,384]{3,0,2,1:T(8,128)S(1)} %get-tuple-element.11, f32[8]{0:T(128)S(1)} %select_reduce_fusion, f32[8,32,384]{2,1,0:T(8,128)S(1)} %copy-done.1, f32[8,14,32,384]{3,0,2,1:T(8,128)S(1)} %maximum_convert_fusion), kind=kLoop, calls=%fused_computation.42 | loop fusion | flops 22020088 | bytes 31064608 | tf_op jit(solution)/shard_map/reduce_sum | solution.py:53
  188.9 23.6 %psum.23 = f32[8]{0:T(128)S(1)} all-reduce(f32[8]{0:T(128)S(1)} %get-tuple-element.8), channel_id=1, replica_groups=mesh['grid'=8,'band'=4] {'grid'}, use_global_device_ids=true, to_apply=%region_5.6 | all-reduce | flops 8 | bytes 64 | tf_op jit(solution)/shard_map/psum | solution.py:99
  212.5 9.1 %multiply_subtract_fusion = (f32[8,8,32,384]{3,0,2,1:T(8,128)S(1)}, f32[8,8,32,384]{3,0,2,1:T(8,128)S(1)}) fusion(f32[8,8,32,384]{3,0,2,1:T(8,128)} %get-tuple-element.9, f32[8,8,32,384]{3,2,1,0:T(8,128)} %param.9, f32[8]{0:T(128)S(1)} %div.36, f32[8,8,32,384]{3,0,2,1:T(8,128)S(1)} %get-tuple-element.11, f32[8,8,32,384]{3,2,1,0:T(8,128)} %param.11), kind=kLoop, calls=%fused_computation.41 | loop fusion | flops 3145728 | bytes 18874400 | tf_op jit(solution)/shard_map/sub | solution.py:101
  221.6 2.2 copy.20
  223.8 2.2 copy.19
  (16 shorter events, 0.0 us)
Async XLA Ops:
  7.2 4.2 %copy-start.2 = (s32[8]{0:T(128)S(1)}, s32[8]{0:T(128)}, u32[]{:S(2)}) copy-start(s32[8]{0:T(128)} %param.16) | copy-start | bytes 100
  7.2 4.3 %copy-start.3 = (f32[32]{0:T(128)S(1)}, f32[32]{0:T(128)}, u32[]{:S(2)}) copy-start(f32[32]{0:T(128)} %param.14) | copy-start | bytes 388
  7.2 121.9 %copy-start.1 = (f32[8,32,384]{2,1,0:T(8,128)S(1)}, f32[8,32,384]{2,1,0:T(8,128)}, u32[]{:S(2)}) copy-start(f32[8,32,384]{2,1,0:T(8,128)} %param.15) | copy-start | bytes 1179652
  7.2 121.9 %copy-start = (f32[8,8,32,384]{3,2,1,0:T(8,128)S(1)}, f32[8,8,32,384]{3,2,1,0:T(8,128)}, u32[]{:S(2)}) copy-start(f32[8,8,32,384]{3,2,1,0:T(8,128)} %param.9) | copy-start | bytes 9437188
  7.2 121.9 %all-gather.2.cloned.1.call-start = ((), (), s32[]{:S(2)}) async-start(), calls=%async_computation | async-start | bytes 7864320 | tf_op jit(solution)/shard_map/all_gather | solution.py:75
  11.6 139.4 %copy-start.4 = (s32[8]{0:T(128)S(1)}, s32[8]{0:T(128)}, u32[]{:S(2)}) copy-start(s32[8]{0:T(128)} %param.17) | copy-start | bytes 100
  151.1 19.7 %copy-start.5 = (f32[8]{0:T(128)S(1)}, f32[8]{0:T(128)}, u32[]{:S(2)}) copy-start(f32[8]{0:T(128)} %param.12) | copy-start | bytes 100
  170.7 41.7 %copy-start.6 = (f32[8]{0:T(128)}, f32[8]{0:T(128)S(1)}, u32[]{:S(2)}) copy-start(f32[8]{0:T(128)S(1)} %psum.22) | copy-start | bytes 100
  176.0 5.3 %collective-permute-start = (bf16[8,3,32,384]{3,0,2,1:T(8,128)(2,1)S(1)}, bf16[8,3,32,384]{3,0,2,1:T(8,128)(2,1)S(1)}, u32[]{:S(2)}, u32[]{:S(2)}) collective-permute-start(bf16[8,3,32,384]{3,0,2,1:T(8,128)(2,1)S(1)} %get-tuple-element.12), channel_id=1, source_target_pairs={{0,4},{4,8},{8,12},{12,16},{16,20},{20,24},{24,28},{1,5},{5,9},{9,... | collective-permute-start | bytes 1769480 | tf_op jit(solution)/shard_map/ppermute | solution.py:20
  177.8 3.9 %collective-permute-start.1 = (bf16[8,3,32,384]{3,0,2,1:T(8,128)(2,1)S(1)}, bf16[8,3,32,384]{3,0,2,1:T(8,128)(2,1)S(1)}, u32[]{:S(2)}, u32[]{:S(2)}) collective-permute-start(bf16[8,3,32,384]{3,0,2,1:T(8,128)(2,1)S(1)} %get-tuple-element.13), channel_id=1, source_target_pairs={{4,0},{8,4},{12,8},{16,12},{20,16},{24,20},{28,24},{5,1},{9,5},{13... | collective-permute-start | bytes 1769480 | tf_op jit(solution)/shard_map/ppermute | solution.py:22
Sparse Core Ops, SparseCore 0:
  11.0 118.0 all-gather.1
where the time goes:
time: 233 us
  waiting for transfers between devices  118 us (51%)
  blocking collectives  49.3 us (21%)
  other arithmetic  22.1 us (9%)
  matrix products  15.9 us (7%)
  between operations  14.1 us (6%)
  local copies, waits for them, and re-layouts  10.5 us (5%)
  starting transfers between devices  3.13 us (1%)
    all_gather x1, waiting for transfers between devices, on_device(): wave = lax.all_gather(orbitals, 'band', axis=0, tiled=True)  117 us
    psum x1, blocking collectives, on_device(): curvature = lax.psum(cell_sum(new_dir, image), 'grid')  23.6 us
    psum x1, blocking collectives, on_device(): correlation = lax.psum(correlation_local, 'grid')  13.8 us
    psum x1, blocking collectives, on_device(): rr_now = lax.psum(cell_sum(residual, projected), 'grid')  11.9 us
    unnamed x18, local copies, waits for them, and re-layouts  10.3 us
    sub x1, other arithmetic, on_device(): residual - step_size * image  9.1 us
    dot_general x1, matrix products, on_device(): jnp.einsum('cxyz,bxyz->cb', start, wave, precision=lax.Precision.HIGHEST,...  8.12 us
    dot_general x1, matrix products, on_device(): jnp.einsum('cb,bxyz->cxyz', chosen, wave, precision=lax.Precision.HIGHEST...  7.77 us
  transfers between devices with their start and end apart: 3, of which 2 were waited for; matrix products, arithmetic and copies ran while one was open for 1% of the time, Pallas kernels for 0%

commit v1 on v0

v1 whole, which is shorter than its diff:
```python
import functools

import jax
import jax.numpy as jnp
from jax import lax
from jax.experimental import pallas as pl
from jax.experimental.pallas import tpu as pltpu
from jax.sharding import PartitionSpec as P

PB = 16
K0 = -49.0 / 18.0
SIDE = (270.0, -27.0, 2.0)
SCALE = -0.5 / 180.0
F32, BF16 = jnp.float32, jnp.bfloat16
TILE = 16
MIB = 1 << 20
TOP = 16384.0
NT = (((1,), (1,)), ((), ()))
LANE_S, LANE_R, LANE_RS, LANE_CAP = 0, 32, 96, 100


def edge_plane(i):
    return i + 2 * (i // 3)


def high_plane(i):
    return i + 5


def mid_plane(i):
    return i + 3


def same_plane(i):
    return i


def plane_spec(shape, place, part=0):
    return pl.BlockSpec((shape[0], 1) + tuple(shape[2:]), lambda i: (part, place(i), 0, 0))


def piece(array, size, part, first=0):
    return array, (size,) + tuple(array.shape[1:]), part, first


def as_piece(x):
    return x if isinstance(x, tuple) else piece(x, x.shape[0], 0)


def piece_spec(x, planes, place):
    array, shape, part, first = x
    return plane_spec(shape, place if shape[1] == planes else (lambda i: i + first), part)


def whole_spec(shape):
    return pl.BlockSpec(tuple(shape), lambda i: (0,) * len(shape))


def params(limit):
    return pltpu.CompilerParams(vmem_limit_bytes=limit * MIB)


CHEAP = pl.CostEstimate(flops=10**6, bytes_accessed=MIB, transcendentals=0)


DIRECT = pl.BlockSpec(memory_space=pltpu.VMEM)


def near(shape, dtype):
    return pltpu.VMEM(tuple(shape), dtype)


def far(x):
    return pltpu.with_memory_space_constraint(x, pltpu.HBM)


def held(x):
    return pltpu.with_memory_space_constraint(x, pltpu.VMEM)


def dot(a, b):
    return jnp.dot(a, b, preferred_element_type=F32)


def exact_dot(a, b):
    return jnp.dot(a, b, precision=lax.Precision.HIGHEST, preferred_element_type=F32)


def split(x):
    high = x.astype(BF16)
    return high, (x - high.astype(F32)).astype(BF16)


def in_lane(column, lane):
    at = lax.broadcasted_iota(jnp.int32, (column.shape[0], 128), 1)
    return jnp.where(at == lane, column, 0.0)


def prepare_kernel(planes, r_ref, d_ref, v_ref, e_ref, o_ref, s_ref, keep_ref, lhs_ref, give_ref, sum_ref, total):
    i = pl.program_id(0)
    count = r_ref.shape[0]

    @pl.when(i == 0)
    def _():
        total[...] = jnp.zeros_like(total)

    r = r_ref[:, 0]
    s = r / (v_ref[0][None] - e_ref[:, 0:1][:, :, None] - 1.5 * K0)
    s_ref[:, i] = s
    keep_ref[:, i] = d_ref[:, 0]
    short = s.astype(BF16)
    lhs_ref[:count, 0] = short
    lhs_ref[count:, 0] = r.astype(BF16)
    total[...] += jnp.sum(r * s, axis=1)

    @pl.when((i == planes // 2 - 1) | (i == planes // 2))
    def _():
        give_ref[:count, 0] = short
        give_ref[count : 2 * count, 0] = r.astype(BF16)
        give_ref[2 * count :] = o_ref[...]

    @pl.when(i == planes - 1)
    def _():
        sum_ref[:count] = jnp.zeros((count, 128), F32)
        sum_ref[count:] = in_lane(jnp.sum(total[...], axis=1, keepdims=True), LANE_RS)


def prepare(residual, direction, potential, energy, mid):
    shape = residual.shape
    count, planes, rows, depth = shape
    cut = lambda fields, size: (fields, size) + tuple(shape[2:])
    middle = lambda i: jnp.clip(i - 3, 0, 1)
    outs = [cut(2 * count, planes), cut(2 * count + mid.shape[0], 2)]
    maps = [same_plane, middle]
    return pl.pallas_call(
        functools.partial(prepare_kernel, planes),
        grid=(planes,),
        in_specs=[
            plane_spec(shape, same_plane),
            plane_spec(shape, same_plane),
            pl.BlockSpec((1, rows, depth), lambda i: (i, 0, 0)),
            whole_spec(energy.shape),
            plane_spec(mid.shape, middle),
        ],
        out_specs=[DIRECT] * 2 + [plane_spec(o, m) for o, m in zip(outs, maps)] + [whole_spec((2 * count, 128))],
        out_shape=[near(shape, F32)] * 2 + [near(o, BF16) for o in outs] + [jax.ShapeDtypeStruct((2 * count, 128), F32)],
        scratch_shapes=[pltpu.VMEM((count, depth), F32)],
        compiler_params=params(8),
        cost_estimate=CHEAP,
        name="prepare",
    )(far(residual), far(direction), far(potential), energy, mid)


def corr_kernel(slots, offsets, steps, lefts, arity, sums_in, capped, masked, *refs):
    prevs, refs = refs[:sums_in], refs[sums_in:]
    if masked:
        mask_ref, refs = refs[0], refs[1:]
    lhs, refs = refs[:lefts], refs[lefts:]
    terms, out_ref, acc, top = refs[:arity], refs[arity], refs[arity + 1], refs[arity + 2]
    i = pl.program_id(0)

    @pl.when(i == 0)
    def _():
        acc[...] = jnp.zeros_like(acc)
        top[...] = jnp.zeros_like(top)

    bands = terms[0].shape[0]
    rows, depth = terms[0].shape[2], terms[0].shape[3]
    for y in range(0, rows, TILE):
        at = lambda r: r[:, 0, y : y + TILE, :].reshape(r.shape[0] * TILE, depth)
        right = jnp.concatenate([at(t) for t in terms], axis=0)
        if capped:
            size = jnp.max(jnp.abs(right.astype(F32)), axis=0, keepdims=True)
            top[...] = jnp.maximum(top[...], jnp.broadcast_to(size, top.shape))
        row = 0
        for ref in lhs:
            size = ref.shape[0] * TILE
            acc[row : row + size, :] += lax.dot_general(at(ref), right, NT, preferred_element_type=F32)
            row += size

    @pl.when(i == steps - 1)
    def _():
        width = acc.shape[1]
        row = lax.broadcasted_iota(jnp.int32, acc.shape, 0)
        col = lax.broadcasted_iota(jnp.int32, acc.shape, 1)
        same = jnp.where((row & (TILE - 1)) == (col & (TILE - 1)), acc[...], 0.0)
        red = jnp.sum(same.reshape(acc.shape[0] // TILE, TILE, width), axis=1)
        src = lax.broadcasted_iota(jnp.int32, (width, 128), 0)
        dst = lax.broadcasted_iota(jnp.int32, (width, 128), 1)
        band = src // TILE
        goal = jnp.full_like(band, -1000)
        for number, slot in enumerate(slots):
            goal = jnp.where(band // bands == number, slot * bands + band % bands, goal)
        total = prevs[0][...]
        for prev in prevs[1:]:
            total = total + prev[...]
        out_ref[...] = total
        per = red.shape[0] // len(offsets)
        for number, (top_row, lane) in enumerate(offsets):
            place = jnp.where(goal + lane == dst, 1.0, 0.0).astype(F32)
            out_ref[top_row : top_row + per, :] += exact_dot(red[number * per : (number + 1) * per], place)
        if capped:
            most = jnp.max(top[...], axis=1, keepdims=True)
            out_ref[per : 2 * per, :] += in_lane(most, LANE_CAP)
        if masked:
            out_ref[:per, :] = out_ref[:per, :] * mask_ref[...]


def correlate(prevs, lhs, offsets, terms, slots, place, steps, capped=False, mask=None):
    lhs, terms = [as_piece(a) for a in lhs], [as_piece(t) for t in terms]
    spec = lambda a: piece_spec(a, 8, place)
    fields, bands = sum(a[1][0] for a in lhs), terms[0][1][0]
    small = list(prevs) + ([] if mask is None else [mask])
    return pl.pallas_call(
        functools.partial(
            corr_kernel, slots, offsets, steps, len(lhs), len(terms), len(prevs), capped, mask is not None
        ),
        grid=(steps,),
        in_specs=[whole_spec(p.shape) for p in small] + [spec(a) for a in [*lhs, *terms]],
        out_specs=whole_spec(prevs[0].shape),
        out_shape=jax.ShapeDtypeStruct(prevs[0].shape, F32),
        scratch_shapes=[
            pltpu.VMEM((fields * TILE, len(terms) * bands * TILE), F32),
            pltpu.VMEM((8, terms[0][1][3]), F32),
        ],
        compiler_params=params(10),
        cost_estimate=CHEAP,
        name="correlate",
    )(*small, *[a[0] for a in lhs], *[t[0] for t in terms])


def band_matrix(size, period):
    row = lax.broadcasted_iota(jnp.int32, (size, size), 0)
    col = lax.broadcasted_iota(jnp.int32, (size, size), 1)
    away = jnp.abs(row - col)
    value = jnp.where(away == 1, SIDE[0], jnp.where(away == 2, SIDE[1], jnp.where(away == 3, SIDE[2], 0.0)))
    return jnp.where(row // period == col // period, value, 0.0).astype(BF16)


def coefficients(tot_ref, count):
    lane = lax.broadcasted_iota(jnp.int32, (count, 128), 1)
    return jnp.where(lane < LANE_R, tot_ref[:count], 0.0)


def scalars(tot_ref, info_ref):
    count = info_ref.shape[0]
    raw = tot_ref[:count, LANE_S : LANE_S + 32]
    product = tot_ref[count : 2 * count, LANE_RS : LANE_RS + 1]
    product = product - jnp.sum(raw * tot_ref[:count, LANE_R : LANE_R + 32], axis=1, keepdims=True)
    return product, product / info_ref[:, 0:1]


def widened(chosen, w_ref):
    count, width = chosen.shape[0], w_ref.shape[1]
    src = lax.broadcasted_iota(jnp.int32, (128, width), 0)
    dst = lax.broadcasted_iota(jnp.int32, (128, width), 1)
    spread = jnp.where(src == dst // TILE, 1.0, 0.0).astype(BF16)
    row = lax.broadcasted_iota(jnp.int32, (count, TILE, width), 1)
    col = lax.broadcasted_iota(jnp.int32, (count, TILE, width), 2)
    for half, part in enumerate(split(chosen)):
        wide = jnp.broadcast_to(dot(part, spread)[:, None, :], (count, TILE, width))
        kron = jnp.where(row == (col & (TILE - 1)), wide, 0.0)
        w_ref[half * count * TILE : (half + 1) * count * TILE, :] = kron.reshape(
            count * TILE, width
        ).astype(BF16)


def combined(w_ref, groups, plane, y):
    every = []
    for group in groups:
        parts = [
            ref[size * part : size * (part + 1), plane + first, y : y + TILE, :] for ref, size, part, first in group
        ]
        whole = parts[0]
        for part in parts[1:]:
            whole = whole + part
        every.append(whole.reshape(whole.shape[0] * TILE, whole.shape[2]))
    both = dot(w_ref[...], jnp.concatenate(every, axis=0))
    half = both.shape[0] // 2
    return (both[:half] + both[half:]).reshape(half // TILE, TILE, both.shape[1])


def grouped(refs, layout):
    groups, at = [], 0
    for group in layout:
        groups.append([(refs[at + number], *where) for number, where in enumerate(group)])
        at += len(group)
    return groups, refs[at:]


def laid_out(slots):
    flat = [as_piece(o) for group in slots for o in group]
    layout, at = [], 0
    for group in slots:
        layout.append([(o[1][0], o[2], o[3]) for o in flat[at : at + len(group)]])
        at += len(group)
    return [held(o[0]) for o in flat], layout


def direction_kernel(layout, edges, base, aliased, tot_ref, info_ref, s_ref, d_ref, *rest):
    groups, rest = grouped(rest, layout)
    if not edges:
        (lost_ref, cap_ref), rest = rest[:2], rest[2:]
    n_ref, rest = rest[aliased], rest[aliased + 1 :]
    if edges:
        side_ref, rr_ref, rest = rest[0], rest[1], rest[2:]
    w_ref, scale_ref = rest
    i = pl.program_id(0)
    count = info_ref.shape[0]

    @pl.when(i == 0)
    def _():
        product, beta = scalars(tot_ref, info_ref)
        chosen = coefficients(tot_ref, count)
        scale_ref[0] = jnp.broadcast_to(beta, scale_ref.shape[1:])
        if edges:
            rr_ref[...] = jnp.broadcast_to(product, rr_ref.shape)
        else:
            scale_ref[1] = jnp.broadcast_to(reach(chosen, cap_ref), scale_ref.shape[1:])
            chosen = chosen * info_ref[:, 2:3]
        widened(chosen, w_ref)

    beta = scale_ref[0][:, 0:1][:, :, None]
    for y in range(0, s_ref.shape[2], TILE):
        part = slice(y, y + TILE)
        new = s_ref[:, base - 3 + i, part, :] - combined(w_ref, groups, i, y)
        new = new + beta * d_ref[:, base - 3 + i, part, :]
        if edges:
            side_ref[:, 0, part, :] = new.astype(BF16)
        else:
            new = new - scale_ref[1][:, 0:1][:, :, None] * lost_ref[:, 0, part, :]
        n_ref[:, base + i, part, :] = new


def directions(tot, info, start, direction, slots, steps, base, so_far=None, lost=None, cap=None):
    shape = start.shape
    edges = lost is None
    wide = (shape[0], shape[1] + 6) + tuple(shape[2:])
    part = (shape[0], steps) + tuple(shape[2:])
    flat, layout = laid_out(slots)
    args = [tot, info, held(start), held(direction), *flat]
    in_specs = [whole_spec(tot.shape), whole_spec(info.shape)] + [DIRECT] * (2 + len(flat))
    if not edges:
        args += [lost, cap]
        in_specs += [plane_spec(part, same_plane), whole_spec(cap.shape)]
    aliases = {}
    if so_far is not None:
        aliases = {len(args): 0}
        args.append(held(so_far))
        in_specs.append(DIRECT)
    out_specs = [DIRECT]
    out_shape = [near(wide, F32)]
    if edges:
        out_specs += [plane_spec(part, same_plane), whole_spec(info.shape)]
        out_shape += [near(part, BF16), jax.ShapeDtypeStruct(info.shape, F32)]
    work = 3 if edges else 64
    return pl.pallas_call(
        functools.partial(direction_kernel, layout, edges, base, len(aliases)),
        grid=(steps,),
        in_specs=in_specs,
        out_specs=out_specs,
        out_shape=out_shape,
        input_output_aliases=aliases,
        scratch_shapes=[
            pltpu.VMEM((2 * shape[0] * TILE, len(slots) * layout[0][0][0] * TILE), BF16),
            pltpu.VMEM((2, shape[0], 128), F32),
        ],
        compiler_params=params(6),
        cost_estimate=pl.CostEstimate(
            flops=steps * 2 * 256 * 1024 * 384, bytes_accessed=work * MIB, transcendentals=0
        ),
        name="directions",
    )(*args)


def reach(chosen, cap_ref):
    count = chosen.shape[0]
    cap = cap_ref[count : 2 * count, LANE_CAP : LANE_CAP + 1]
    return jnp.maximum(jnp.sum(jnp.abs(chosen), axis=1, keepdims=True) * cap, 1e-30)


def removal_kernel(layout, tot_ref, cap_ref, *rest):
    groups, (out_ref, w_ref) = grouped(rest, layout)

    @pl.when(pl.program_id(0) == 0)
    def _():
        chosen = coefficients(tot_ref, out_ref.shape[0])
        widened(chosen / reach(chosen, cap_ref), w_ref)

    for y in range(0, out_ref.shape[2], TILE):
        out_ref[:, 0, y : y + TILE, :] = combined(w_ref, groups, pl.program_id(0), y)


def removals(tot, cap, slots, count):
    flat, layout = laid_out(slots)
    shape = (count,) + tuple(as_piece(slots[0][0])[1][1:])
    return pl.pallas_call(
        functools.partial(removal_kernel, layout),
        grid=(shape[1],),
        in_specs=[whole_spec(tot.shape), whole_spec(cap.shape)] + [DIRECT] * len(flat),
        out_specs=plane_spec(shape, same_plane),
        out_shape=near(shape, F32),
        scratch_shapes=[
            pltpu.VMEM((2 * count * TILE, len(slots) * layout[0][0][0] * TILE), BF16),
        ],
        compiler_params=params(6),
        cost_estimate=pl.CostEstimate(
            flops=2 * 2 * 256 * 1024 * 384, bytes_accessed=4 * MIB, transcendentals=0
        ),
        name="removals",
    )(tot, cap, *flat)


def image_kernel(
    planes, info_ref, low_ref, high_ref, v_ref, wide_in, r_ref, x_ref,
    new_ref, image_ref, curve_ref, keep_ref, n_ref, r_near, x_near, ky, even, odd, total, sem,
):
    i = pl.program_id(0)
    count, _, rows, depth = n_ref.shape

    @pl.when(i == 0)
    def _():
        ky[...] = band_matrix(count * rows, rows)
        total[...] = jnp.zeros_like(total)
        pltpu.make_async_copy(r_ref, r_near, sem.at[0]).start()
        pltpu.make_async_copy(x_ref, x_near, sem.at[1]).start()
        n_ref[:, 0:3] = low_ref[...].astype(F32)
        n_ref[:, planes + 3 : planes + 6] = high_ref[...].astype(F32)

    lane = lax.broadcasted_iota(jnp.int32, (rows, depth), 1)
    for half, beside in enumerate((even, odd)):
        high, low = split(n_ref[:, 2 * i + half + 3].reshape(count * rows, depth))
        beside[...] = (dot(ky[...], high) + dot(ky[...], low)).reshape(beside.shape)
    for half, beside in enumerate((even, odd)):
        plane = 2 * i + half + 3
        shifted = v_ref[half] - 1.5 * K0
        for c in range(count):
            here = n_ref[c, plane]
            side = beside[c]
            for away in range(1, 4):
                below = jnp.where(lane >= away, pltpu.roll(here, away, 1), 0.0)
                above = jnp.where(lane < depth - away, pltpu.roll(here, depth - away, 1), 0.0)
                pair = n_ref[c, plane - away] + n_ref[c, plane + away]
                side = side + SIDE[away - 1] * (below + above + pair)
            image = SCALE * side + (shifted - info_ref[c : c + 1, 1:2]) * here
            new_ref[c, half] = here
            keep_ref[c, plane - 3] = here
            image_ref[c, plane - 3] = image
            total[c : c + 1] += jnp.sum(here * image, axis=0, keepdims=True)

    @pl.when(i == planes // 2 - 1)
    def _():
        curve_ref[...] = jnp.broadcast_to(jnp.sum(total[...], axis=1, keepdims=True), curve_ref.shape)
        pltpu.make_async_copy(r_ref, r_near, sem.at[0]).wait()
        pltpu.make_async_copy(x_ref, x_near, sem.at[1]).wait()


def images(info, low, wide, high, potential, residual, solution):
    count, _, rows, depth = wide.shape
    planes = potential.shape[0]
    shape = (count, planes, rows, depth)
    return pl.pallas_call(
        functools.partial(image_kernel, planes),
        grid=(planes // 2,),
        in_specs=[
            whole_spec(info.shape), DIRECT, DIRECT,
            pl.BlockSpec((2, rows, depth), lambda i: (i, 0, 0)),
            DIRECT,
        ]
        + [pl.BlockSpec(memory_space=pl.ANY)] * 2,
        out_specs=[
            pl.BlockSpec((count, 2, rows, depth), lambda i: (0, i, 0, 0)), DIRECT, whole_spec((count, 128)),
        ]
        + [DIRECT] * 4,
        out_shape=[
            pltpu.HBM(shape, F32), near(shape, F32), jax.ShapeDtypeStruct((count, 128), F32),
            near(shape, F32), near(wide.shape, F32), near(shape, F32), near(shape, F32),
        ],
        input_output_aliases={4: 4},
        scratch_shapes=[
            pltpu.VMEM((count * rows, count * rows), BF16),
            pltpu.VMEM((count, rows, depth), F32),
            pltpu.VMEM((count, rows, depth), F32),
            pltpu.VMEM((count, depth), F32),
            pltpu.SemaphoreType.DMA((2,)),
        ],
        compiler_params=params(8),
        cost_estimate=pl.CostEstimate(flops=4 * 10**9, bytes_accessed=24 * MIB, transcendentals=0),
        name="images",
    )(info, held(low), held(high), far(potential), held(wide), far(residual), far(solution))


def finish_kernel(planes, tot_ref, info_ref, curve_ref, n_ref, image_ref, r_ref, x_ref, sol_ref, res_ref, sol, res, sem):
    product, _ = scalars(tot_ref, info_ref)
    size = jnp.broadcast_to(product / curve_ref[:, 0:1], info_ref.shape)[:, 0:1][:, :, None]
    copies = []
    for plane in range(planes):
        sol[:, plane] = x_ref[:, plane] + size * n_ref[:, plane]
        res[:, plane] = r_ref[:, plane] - size * image_ref[:, plane]
        for number, (source, target) in enumerate(((sol, sol_ref), (res, res_ref))):
            copy = pltpu.make_async_copy(source.at[:, plane], target.at[:, plane], sem.at[number, plane])
            copy.start()
            copies.append(copy)
    for copy in copies:
        copy.wait()


def finish(tot, info, curve, new, image, residual, solution):
    shape = new.shape
    return pl.pallas_call(
        functools.partial(finish_kernel, shape[1]),
        in_specs=[DIRECT] * 7,
        out_specs=[pl.BlockSpec(memory_space=pl.ANY)] * 2,
        out_shape=[pltpu.HBM(shape, F32)] * 2,
        scratch_shapes=[pltpu.VMEM(shape, F32)] * 2 + [pltpu.SemaphoreType.DMA((2, shape[1]))],
        compiler_params=params(8),
        name="finish",
    )(tot, info, curve, held(new), held(image), held(residual), held(solution))


def after(value, *others):
    return lax.optimization_barrier((value, *others))[0]


SWAP = [(0, 1), (1, 0), (2, 3), (3, 2)]
INNER = [(1, 2), (2, 1)]
INWARD = [(0, 1), (3, 2)]
OUTWARD = [(1, 0), (2, 3)]


def grid_sum(value):
    size = lax.axis_size("grid")
    away = lambda x, step: lax.ppermute(x, "grid", [(i, i ^ step) for i in range(size)])
    value = value + away(value, 1)
    stride = 2
    while stride < size:
        if 4 * stride <= size:
            near_by, above, across = (away(value, step * stride) for step in (1, 2, 3))
            value = (value + near_by) + (above + across)
            stride *= 4
        else:
            value = value + away(value, stride)
            stride *= 2
    return value


def hop(value, pairs):
    return lax.ppermute(value, "band", pairs)


def on_device(
    residual,
    direction,
    solution,
    old_product,
    orbitals,
    energies,
    potential,
    column_index,
    panel_index,
):
    count = residual.shape[0]
    bands = orbitals.shape[0]
    groups = lax.axis_size("band")
    place = lax.axis_index("band")
    is_end = (place == 0) | (place == groups - 1)
    ends = lax.axis_size("grid") - 1
    upward = [(i, i + 1) for i in range(ends)]
    downward = [(i + 1, i) for i in range(ends)]
    used = groups * bands

    halves = (orbitals[:, 0:3], orbitals[:, 5:8])
    mid = orbitals[:, 3:5]
    edge_pair = [hop(half, SWAP) for half in halves]
    edge_inner = hop(jnp.concatenate(halves, axis=1), INNER)
    sides = lambda x: [piece(x, bands, 0, 0), piece(x, bands, 0, 3)]

    band_ids = lax.iota(jnp.int32, energies.shape[0])
    picked = jnp.where(
        band_ids[None, :] == (column_index // 3)[:, None], energies[None, :], jnp.float32(0.0)
    )
    energy = jnp.sum(picked, axis=1)
    wide_energy = jnp.broadcast_to(energy[:, None], (count, 128))
    start, direction, lhs, give, tot = prepare(residual, direction, potential, wide_energy, mid)
    lhs = held(lhs)
    kinds = ((0, LANE_S), (0, LANE_R))
    places = (same_plane, high_plane)
    tot = correlate([tot], [lhs], kinds, [far(orbitals)], (0,), edge_plane, 6)

    edge_far = [hop(after(half, tot), INNER) for half in edge_pair]
    edge_next = hop(after(edge_inner, tot), OUTWARD)
    got = hop(give, INWARD)
    for pair, inner, where in zip(edge_pair, sides(edge_inner), places):
        tot = correlate([tot], [lhs], kinds, [pair, inner], (1, 2), where, 3)

    edge_last = [hop(after(edge_far[0], tot), OUTWARD), hop(after(edge_far[1], tot, edge_next), OUTWARD)]
    both = hop(jnp.concatenate([mid, after(got, tot, *edge_far)[2 * count :]]), INNER)
    mid_pair, mid_inner, mid_far = piece(got, bands, 2 * count // bands), piece(both, bands, 0), piece(both, bands, 1)
    mids = [mid, mid_pair, mid_inner, mid_far]
    for nearer, farther, where in zip(sides(edge_next), edge_far, places):
        tot = correlate([tot], [lhs], kinds, [nearer, farther], (2, 3), where, 3)
    given = correlate(
        [jnp.zeros((2 * count, 128), F32)], [piece(got, 2 * count, 0)], kinds,
        [mid, mid_inner, mid_far, mid_pair], (1, 2, 3, -100), same_plane, 2, True,
    )
    tot = correlate([tot], [lhs], kinds, mids, (0, 1, 2, 3), mid_plane, 2)
    taken = hop(after(given, tot), OUTWARD)
    tot = correlate([tot], [lhs], kinds, [edge_last[0]], (3,), same_plane, 3)

    lane = lax.iota(jnp.int32, 128)
    group = jnp.where(
        place < groups // 2,
        jnp.stack([place, 1 - place, jnp.int32(2), jnp.int32(3)]),
        jnp.stack([place, 5 - place, jnp.int32(1), jnp.int32(0)]),
    )
    ids = (group[:, None] * bands + lax.iota(jnp.int32, bands)[None, :]).reshape(used)
    cells = float(residual.shape[1] * lax.axis_size("grid") * residual.shape[2] * residual.shape[3])
    member = jnp.where(ids[None, :] // PB == panel_index[:, None], jnp.float32(1.0 / cells), jnp.float32(0.0))
    member = jnp.pad(member, ((0, 0), (0, 128 - used)), constant_values=1.0)
    inside = jnp.where(is_end, 0.0, 1.0)
    info = jnp.where(
        lane[None, :] == 0,
        old_product[:, None],
        jnp.where(lane[None, :] == 1, energy[:, None], inside),
    )
    cap = given * inside + taken
    tot, cap, info, member = lax.optimization_barrier((tot, cap, info, member))
    tot = correlate([tot, taken], [lhs], kinds, [edge_last[1]], (3,), high_plane, 3, False, member)
    tot = grid_sum(tot)

    slots = [
        [[halves[half]], [edge_pair[half]], [inner, nearer], [edge_far[half], edge_last[half]]]
        for half, inner, nearer in zip(range(2), sides(edge_inner), sides(edge_next))
    ]
    other_tot = hop(tot, INWARD)
    wide, low, product = directions(tot, info, start, direction, slots[0], 3, 3)
    from_right = lax.ppermute(low, "grid", downward)
    lost = removals(after(other_tot, low), cap, [[mid_pair], [mid], [mid_inner], [mid_far]], count)
    lost = (lost * jnp.float32(TOP)).astype(jnp.float16)
    wide, high, _ = directions(after(tot, lost), info, start, direction, slots[1], 3, 8, wide)
    from_left = lax.ppermute(high, "grid", upward)
    lost = hop(lost, OUTWARD).astype(F32) * jnp.float32(1.0 / TOP)
    (wide,) = directions(
        tot, info, start, direction, [[m] for m in mids], 2, 6, wide, lost, cap
    )
    new, image, curve, keep, _, residual, solution = images(
        info, from_left, wide, from_right, potential, residual, solution
    )
    curve = grid_sum(curve)
    new_solution, new_residual = finish(tot, info, curve, keep, image, residual, solution)
    return new_solution, new_residual, new, product[:, 0]


def solution(mesh):
    tiles = P("band", "grid", None, None)
    return jax.shard_map(
        on_device,
        mesh=mesh,
        in_specs=(tiles, tiles, tiles, P("band"), tiles, P(), P("grid", None, None), P("band"), P("band")),
        out_specs=(tiles, tiles, tiles, P("band")),
        check_vma=False,
    )
```

time: 233 us -> 156 us (0.67)
  waiting for transfers between devices: 118 us -> 44.7 us
  Pallas kernels: 0 us -> 58 us
  blocking collectives: 49.3 us -> 0 us
  starting transfers between devices: 3.13 us -> 41.1 us
  other arithmetic: 22.1 us -> 2.49 us
  matrix products: 15.9 us -> 0 us
  between operations: 14.1 us -> 1.17 us
  local copies, waits for them, and re-layouts: 10.5 us -> 7.61 us
    all_gather x1 -> x0, waiting for transfers between devices: 117 us -> none  [on_device(): wave = lax.all_gather(orbitals, 'band', axis=0, tiled=True)]
    pallas_call x0 -> x16, Pallas kernels: none -> 58 us  [the longest x9 24.9 us: correlate(): pl.pallas_call(functools.partial(corr_kernel, slots, offsets, steps, len(...]
    psum x3 -> x0, blocking collectives: 49.3 us -> none  [the longest x1 23.6 us: on_device(): curvature = lax.psum(cell_sum(new_dir, image), 'grid')]
    ppermute x2 -> x23, waiting for transfers between devices: 0.37 us -> 44.7 us  [the longest x13 38 us: hop(): return lax.ppermute(value, 'band', pairs)]
    ppermute x2 -> x23, starting transfers between devices: 3.1 us -> 41.1 us  [the longest x13 24.3 us: hop(): return lax.ppermute(value, 'band', pairs)]
    dot_general x2 -> x0, matrix products: 15.9 us -> none  [the longest x1 8.12 us: on_device(): jnp.einsum('cxyz,bxyz->cb', start, wave, precision=lax.Precision.HIGHEST,...]
    sub x1 -> x0, other arithmetic: 9.1 us -> none  [on_device(): residual - step_size * image]
    unnamed x18 -> x24, local copies, waits for them, and re-layouts: 10.3 us -> 3.36 us
  transfers between devices with their start and end apart: 3 -> 23, of which waited for: 2 -> 13; matrix products, arithmetic and copies ran while one was open for 1% -> 3% of each run, Pallas kernels for 0% -> 27%
where the time goes in v1:
time: 156 us; the launch traced here: 155 us
  Pallas kernels  58 us (37%)
  waiting for transfers between devices  44.7 us (29%)
  starting transfers between devices  41.1 us (26%)
  local copies, waits for them, and re-layouts  7.61 us (5%)
  other arithmetic  2.49 us (2%)
    ppermute x13, waiting for transfers between devices, hop(): return lax.ppermute(value, 'band', pairs)  38 us
    pallas_call x9, Pallas kernels, correlate(): pl.pallas_call(functools.partial(corr_kernel, slots, offsets, steps, len(...  24.9 us
    ppermute x13, starting transfers between devices, hop(): return lax.ppermute(value, 'band', pairs)  24.3 us
    ppermute x8, starting transfers between devices, grid_sum(): lax.ppermute(x, 'grid', [(i, i ^ step) for i in range(size)])  12.3 us
    pallas_call x3, Pallas kernels, directions(): pl.pallas_call(functools.partial(direction_kernel, layout, edges, base, l...  10.8 us
    pallas_call x1, Pallas kernels, images(): pl.pallas_call(functools.partial(image_kernel, planes), grid=(planes // 2...  8.58 us
    pallas_call x1, Pallas kernels, prepare(): pl.pallas_call(functools.partial(prepare_kernel, planes), grid=(planes,),...  7.6 us
    ppermute x8, waiting for transfers between devices, grid_sum(): lax.ppermute(x, 'grid', [(i, i ^ step) for i in range(size)])  6.63 us
  transfers between devices with their start and end apart: 23, of which 13 were waited for; matrix products, arithmetic and copies ran while one was open for 3% of the time, Pallas kernels for 27%

profile of v1, /device:TPU:0, one launch (start us, length us, event | category | flops | bytes accessed | tf_op | source)
XLA Modules:
  0.0 154.9 jit_solution(7340031298901522096)
XLA Ops:
  3.9 4.9 %collective-permute-start.2 = (bf16[8,3,32,384]{3,2,1,0:T(8,128)(2,1)S(1)}, bf16[8,3,32,384]{3,2,1,0:T(8,128)(2,1)}, u32[]{:S(2)}, u32[]{:S(2)}) collective-permute-start(bf16[8,3,32,384]{3,2,1,0:T(8,128)(2,1)S(1)} %get-tuple-element.66.rest_0_), channel_id=1, source_target_pairs={{0,1},{1,0},{2,3},{3,2},{4,5},{5,4},{6,7},{7,6},{8,9},{9,8},{10,11... | collective-permute-start | bytes 1769480 | tf_op jit(solution)/shard_map/ppermute | solution.py:548
  10.2 7.6 %prepare.1 = (f32[8,8,32,384]{3,2,1,0:T(8,128)S(1)}, f32[8,8,32,384]{3,2,1,0:T(8,128)S(1)}, bf16[16,8,32,384]{3,2,1,0:T(8,128)(2,1)S(1)}, bf16[24,2,32,384]{3,2,1,0:T(8,128)(2,1)}, f32[16,128]{1,0:T(8,128)S(1)}) custom-call(f32[8,8,32,384]{3,2,1,0:T(8,128)} %r_ref.3, f32[8,8,32,384]{3,2,1,0:T(8,128)} %d_ref.1, f32[8,32,384]{2,1,0:T(8,128)} %v_ref.3, ...), custom_call_target="tpu_custom_call" | custom-call | flops 1000000 | bytes 1048576 | tf_op jit(solution)/shard_map/prepare/pallas_call | solution.py:135
  21.1 4.9 %collective-permute-start.6 = (bf16[24,2,32,384]{3,2,1,0:T(8,128)(2,1)}, bf16[24,2,32,384]{3,2,1,0:T(8,128)(2,1)}, u32[]{:S(2)}, u32[]{:S(2)}) collective-permute-start(bf16[24,2,32,384]{3,2,1,0:T(8,128)(2,1)} %get-tuple-element.40), channel_id=1, source_target_pairs={{0,1},{3,2},{4,5},{7,6},{8,9},{11,10},{12,13},{15,14},{16,17},{19,... | collective-permute-start | bytes 3538952 | tf_op jit(solution)/shard_map/ppermute | solution.py:548
  26.0 4.4 %correlate.9.refs_0_ = f32[16,128]{1,0:T(8,128)S(1)} custom-call(f32[16,128]{1,0:T(8,128)S(1)} %get-tuple-element.35.refs_0_, bf16[16,8,32,384]{3,2,1,0:T(8,128)(2,1)S(1)} %get-tuple-element.36.refs_1_.refs_3_, bf16[8,8,32,384]{3,2,1,0:T(8,128)(2,1)} %refs_2_.1), custom_call_target="tpu_custom_call" | custom-call | flops 1000000 | bytes 1048576 | tf_op jit(solution)/shard_map/correlate/pallas_call | solution.py:214
  30.4 4.8 %collective-permute-done.refs_2_.rest_1_ = bf16[8,3,32,384]{3,2,1,0:T(8,128)(2,1)} collective-permute-done((bf16[8,3,32,384]{3,2,1,0:T(8,128)(2,1)S(1)}, bf16[8,3,32,384]{3,2,1,0:T(8,128)(2,1)}, u32[]{:S(2)}, u32[]{:S(2)}) %collective-permute-start) | collective-permute-done | bytes 589856 | tf_op jit(solution)/shard_map/ppermute | solution.py:548
  39.5 3.1 %correlate.10.refs_0_ = f32[16,128]{1,0:T(8,128)S(1)} custom-call(f32[16,128]{1,0:T(8,128)S(1)} %correlate.9.refs_0_, bf16[16,8,32,384]{3,2,1,0:T(8,128)(2,1)S(1)} %get-tuple-element.36.refs_1_.refs_3_, bf16[8,3,32,384]{3,2,1,0:T(8,128)(2,1)} %collective-permute-done.refs_2_.rest_1_, bf16[8,6,32,384]{3,2,1,0:T(8,128)(2,1)} %collective-permute-done.1.refs_3_.rest_2_), custom_call_target="tpu_custom_call" | custom-call | flops 1000000 | bytes 1048576 | tf_op jit(solution)/shard_map/correlate/pallas_call | solution.py:214
  42.6 3.1 %correlate.11.refs_0_ = f32[16,128]{1,0:T(8,128)S(1)} custom-call(f32[16,128]{1,0:T(8,128)S(1)} %correlate.10.refs_0_, bf16[16,8,32,384]{3,2,1,0:T(8,128)(2,1)S(1)} %get-tuple-element.36.refs_1_.refs_3_, bf16[8,3,32,384]{3,2,1,0:T(8,128)(2,1)} %collective-permute-done.2.refs_2_.rest_1_, bf16[8,6,32,384]{3,2,1,0:T(8,128)(2,1)} %collective-permute-done.1.refs_3_.rest_2_), custom_call_target="tpu_custom_call" | custom-call | flops 1000000 | bytes 1048576 | tf_op jit(solution)/shard_map/correlate/pallas_call | solution.py:214
  45.8 13.3 %collective-permute-done.6.refs_3_.refs_1_.refs_5_.rest_0_.rest_1_ = bf16[24,2,32,384]{3,2,1,0:T(8,128)(2,1)} collective-permute-done((bf16[24,2,32,384]{3,2,1,0:T(8,128)(2,1)}, bf16[24,2,32,384]{3,2,1,0:T(8,128)(2,1)}, u32[]{:S(2)}, u32[]{:S(2)}) %collective-permute-start.6) | collective-permute-done | bytes 1179680 | tf_op jit(solution)/shard_map/ppermute | solution.py:548
  65.0 3.0 %collective-permute-done.3.refs_2_.rest_3_ = bf16[8,6,32,384]{3,2,1,0:T(8,128)(2,1)} collective-permute-done((bf16[8,6,32,384]{3,2,1,0:T(8,128)(2,1)}, bf16[8,6,32,384]{3,2,1,0:T(8,128)(2,1)}, u32[]{:S(2)}, u32[]{:S(2)}) %collective-permute-start.3) | collective-permute-done | bytes 1179680 | tf_op jit(solution)/shard_map/ppermute | solution.py:548
  69.3 2.7 %correlate.16 = f32[16,128]{1,0:T(8,128)S(1)} custom-call(f32[16,128]{1,0:T(8,128)S(1)} %broadcast_in_dim.74.refs_0_, bf16[24,2,32,384]{3,2,1,0:T(8,128)(2,1)} %collective-permute-done.6.refs_3_.refs_1_.refs_5_.rest_0_.rest_1_, bf16[8,2,32,384]{3,2,1,0:T(8,128)(2,1)S(1)} %slice.15.o_ref.refs_2_.rest_1_.rest_0_, ...), custom_call_target="tpu_custom_call" | custom-call | flops 1000000 | bytes 1048576 | tf_op jit(solution)/shard_map/correlate/pallas_call | solution.py:214
  72.0 3.1 %correlate.12.refs_0_ = f32[16,128]{1,0:T(8,128)S(1)} custom-call(f32[16,128]{1,0:T(8,128)S(1)} %correlate.11.refs_0_, bf16[16,8,32,384]{3,2,1,0:T(8,128)(2,1)S(1)} %get-tuple-element.36.refs_1_.refs_3_, bf16[8,6,32,384]{3,2,1,0:T(8,128)(2,1)} %collective-permute-done.3.refs_2_.rest_3_, bf16[8,3,32,384]{3,2,1,0:T(8,128)(2,1)} %collective-permute-done.4.refs_3_.rest_4_), custom_call_target="tpu_custom_call" | custom-call | flops 1000000 | bytes 1048576 | tf_op jit(solution)/shard_map/correlate/pallas_call | solution.py:214
  75.1 3.1 %correlate.13.refs_0_ = f32[16,128]{1,0:T(8,128)S(1)} custom-call(f32[16,128]{1,0:T(8,128)S(1)} %correlate.12.refs_0_, bf16[16,8,32,384]{3,2,1,0:T(8,128)(2,1)S(1)} %get-tuple-element.36.refs_1_.refs_3_, bf16[8,6,32,384]{3,2,1,0:T(8,128)(2,1)} %collective-permute-done.3.refs_2_.rest_3_, bf16[8,3,32,384]{3,2,1,0:T(8,128)(2,1)} %collective-permute-done.5.refs_3_.rest_4_), custom_call_target="tpu_custom_call" | custom-call | flops 1000000 | bytes 1048576 | tf_op jit(solution)/shard_map/correlate/pallas_call | solution.py:214
  78.3 2.7 %correlate.14.refs_0_ = f32[16,128]{1,0:T(8,128)S(1)} custom-call(f32[16,128]{1,0:T(8,128)S(1)} %correlate.13.refs_0_, bf16[16,8,32,384]{3,2,1,0:T(8,128)(2,1)S(1)} %get-tuple-element.36.refs_1_.refs_3_, bf16[8,2,32,384]{3,2,1,0:T(8,128)(2,1)S(1)} %slice.15.o_ref.refs_2_.rest_1_.rest_0_, ...), custom_call_target="tpu_custom_call" | custom-call | flops 1000000 | bytes 1048576 | tf_op jit(solution)/shard_map/correlate/pallas_call | solution.py:214
  82.4 3.0 %collective-permute-done.8.refs_2_.rest_5_ = bf16[8,3,32,384]{3,2,1,0:T(8,128)(2,1)S(1)} collective-permute-done((bf16[8,3,32,384]{3,2,1,0:T(8,128)(2,1)}, bf16[8,3,32,384]{3,2,1,0:T(8,128)(2,1)S(1)}, u32[]{:S(2)}, u32[]{:S(2)}) %collective-permute-start.8) | collective-permute-done | bytes 589856 | tf_op jit(solution)/shard_map/ppermute | solution.py:548
  86.6 12.9 %collective-permute-done.9.refs_1_ = f32[16,128]{1,0:T(8,128)S(1)} collective-permute-done((f32[16,128]{1,0:T(8,128)S(1)}, f32[16,128]{1,0:T(8,128)S(1)}, u32[]{:S(2)}, u32[]{:S(2)}) %collective-permute-start.9) | collective-permute-done | bytes 8224 | tf_op jit(solution)/shard_map/ppermute | solution.py:548
  110.4 3.6 %directions.3 = (f32[8,14,32,384]{3,2,1,0:T(8,128)S(1)}, bf16[8,3,32,384]{3,2,1,0:T(8,128)(2,1)S(1)}, f32[8,128]{1,0:T(8,128)S(1)}) custom-call(f32[16,128]{1,0:T(8,128)S(1)} %add_add_fusion.tot_ref, f32[8,128]{1,0:T(8,128)S(1)} %select_select_fusion.info_ref, f32[8,8,32,384]{3,2,1,0:T(8,128)S(1)} %copy-done.1, f32[8,8,32,384]{3,2,1,0:T(8,128)S(1)} %copy-done.3, ...), custom_call_target="tpu_custom_call" | custom-call | flops 603979776 | bytes 3145728 | tf_op jit(solution)/shard_map/directions/pallas_call | solution.py:357
  114.1 3.1 %removals.1 = f32[8,2,32,384]{3,2,1,0:T(8,128)S(1)} custom-call(f32[16,128]{1,0:T(8,128)S(1)} %collective-permute-done.15.tot_ref, f32[16,128]{1,0:T(8,128)S(1)} %multiply_add_fusion.cap_ref.rest_5_, bf16[24,2,32,384]{3,2,1,0:T(8,128)(2,1)} %collective-permute-done.6.refs_3_.refs_1_.refs_5_.rest_0_.rest_1_, ...), custom_call_target="tpu_custom_call" | custom-call | flops 402653184 | bytes 4194304 | tf_op jit(solution)/shard_map/removals/pallas_call | solution.py:397
  119.8 4.2 %directions.4 = (f32[8,14,32,384]{3,2,1,0:T(8,128)S(1)}, bf16[8,3,32,384]{3,2,1,0:T(8,128)(2,1)S(1)}, f32[8,128]{1,0:T(8,128)}) custom-call(f32[16,128]{1,0:T(8,128)S(1)} %add_add_fusion.tot_ref, f32[8,128]{1,0:T(8,128)S(1)} %select_select_fusion.info_ref, f32[8,8,32,384]{3,2,1,0:T(8,128)S(1)} %copy-done.1, ...), custom_call_target="tpu_custom_call", output_to_operand_aliasing={{0}: (10, {})} | custom-call | flops 603979776 | bytes 3145728 | tf_op jit(solution)/shard_map/directions/pallas_call | solution.py:357
  124.0 3.2 %collective-permute-start.16 = (bf16[8,3,32,384]{3,2,1,0:T(8,128)(2,1)S(1)}, bf16[8,3,32,384]{3,2,1,0:T(8,128)(2,1)S(1)}, u32[]{:S(2)}, u32[]{:S(2)}) collective-permute-start(bf16[8,3,32,384]{3,2,1,0:T(8,128)(2,1)S(1)} %get-tuple-element.55), channel_id=1, source_target_pairs={{0,4},{4,8},{8,12},{12,16},{16,20},{20,24},{24,28},{1,5},{5,9},{9,... | collective-permute-start | bytes 1769480 | tf_op jit(solution)/shard_map/ppermute | solution.py:641
  128.4 2.9 %directions.5.wide_in = f32[8,14,32,384]{3,2,1,0:T(8,128)S(1)} custom-call(f32[16,128]{1,0:T(8,128)S(1)} %add_add_fusion.tot_ref, f32[8,128]{1,0:T(8,128)S(1)} %select_select_fusion.info_ref, f32[8,8,32,384]{3,2,1,0:T(8,128)S(1)} %copy-done.1, f32[8,8,32,384]{3,2,1,0:T(8,128)S(1)} %copy-done.3, ...), custom_call_target="tpu_custom_call", output_to_operand_aliasing={{}: (10, {})} | custom-call | flops 402653184 | bytes 67108864 | tf_op jit(solution)/shard_map/directions/pallas_call | solution.py:357
  131.4 8.6 %images.1 = (f32[8,8,32,384]{3,2,1,0:T(8,128)}, f32[8,8,32,384]{3,2,1,0:T(8,128)S(1)}, f32[8,128]{1,0:T(8,128)S(1)}, f32[8,8,32,384]{3,2,1,0:T(8,128)S(1)}, f32[...) custom-call(f32[8,128]{1,0:T(8,128)S(1)} %select_select_fusion.info_, ...), custom_call_target="tpu_custom_call", output_to_operand_aliasing={{4}: (4, {})} | custom-call | flops 4000000000 | bytes 25165824 | tf_op jit(solution)/shard_map/images/pallas_call | solution.py:462
  140.0 2.7 %collective-permute-start.19 = (f32[8,128]{1,0:T(8,128)S(1)}, f32[8,128]{1,0:T(8,128)S(1)}, u32[]{:S(2)}, u32[]{:S(2)}) collective-permute-start(f32[8,128]{1,0:T(8,128)S(1)} %get-tuple-element.57), channel_id=1, source_target_pairs={{0,4},{4,0},{8,12},{12,8},{16,20},{20,16},{24,28},{28,24},{1,5},{5... | collective-permute-start | bytes 12296 | tf_op jit(solution)/shard_map/ppermute | solution.py:533
  143.5 3.9 %collective-permute-start.22 = (f32[8,128]{1,0:T(8,128)S(1)}, f32[8,128]{1,0:T(8,128)S(1)}, u32[]{:S(2)}, u32[]{:S(2)}) collective-permute-start(f32[8,128]{1,0:T(8,128)S(1)} %add.78), channel_id=1, source_target_pairs={{0,24},{4,28},{8,16},{12,20},{16,8},{20,12},{24,0},{28,4},{1,25},{... | collective-permute-start | bytes 12296 | tf_op jit(solution)/shard_map/ppermute | solution.py:533
  151.7 3.1 %finish.1 = (f32[8,8,32,384]{3,2,1,0:T(8,128)}, f32[8,8,32,384]{3,2,1,0:T(8,128)}) custom-call(f32[16,128]{1,0:T(8,128)S(1)} %add_add_fusion.tot_ref, f32[8,128]{1,0:T(8,128)S(1)} %select_select_fusion.info_ref, f32[8,128]{1,0:T(8,128)S(1)} %add_add_fusion.1.curve_ref, f32[8,8,32,384]{3,2,1,0:T(8,128)S(1)} %get-tuple-element.58.n_ref, ...), custom_call_target="tpu_custom_call" | custom-call | tf_op jit(solution)/shard_map/finish/pallas_call | solution.py:510
  (87 shorter events, 41.8 us)
Async XLA Ops:
  2.2 36.0 %collective-permute-start.1 = (bf16[8,6,32,384]{3,2,1,0:T(8,128)(2,1)S(1)}, bf16[8,6,32,384]{3,2,1,0:T(8,128)(2,1)}, u32[]{:S(2)}, u32[]{:S(2)}) collective-permute-start(bf16[8,6,32,384]{3,2,1,0:T(8,128)(2,1)S(1)} %pad_maximum_fusion), channel_id=1, source_target_pairs={{1,2},{2,1},{5,6},{6,5},{9,10},{10,9},{13,14},{14,13},{17,18},{18,... | collective-permute-start | bytes 3538952 | tf_op jit(solution)/shard_map/ppermute | solution.py:548
  3.9 26.5 %collective-permute-start.2 = (bf16[8,3,32,384]{3,2,1,0:T(8,128)(2,1)S(1)}, bf16[8,3,32,384]{3,2,1,0:T(8,128)(2,1)}, u32[]{:S(2)}, u32[]{:S(2)}) collective-permute-start(bf16[8,3,32,384]{3,2,1,0:T(8,128)(2,1)S(1)} %get-tuple-element.66.rest_0_), channel_id=1, source_target_pairs={{0,1},{1,0},{2,3},{3,2},{4,5},{5,4},{6,7},{7,6},{8,9},{9,8},{10,11... | collective-permute-start | bytes 1769480 | tf_op jit(solution)/shard_map/ppermute | solution.py:548
  8.8 26.4 %collective-permute-start = (bf16[8,3,32,384]{3,2,1,0:T(8,128)(2,1)S(1)}, bf16[8,3,32,384]{3,2,1,0:T(8,128)(2,1)}, u32[]{:S(2)}, u32[]{:S(2)}) collective-permute-start(bf16[8,3,32,384]{3,2,1,0:T(8,128)(2,1)S(1)} %get-tuple-element.67.rest_0_), channel_id=1, source_target_pairs={{0,1},{1,0},{2,3},{3,2},{4,5},{5,4},{6,7},{7,6},{8,9},{9,8},{10,11... | collective-permute-start | bytes 1769480 | tf_op jit(solution)/shard_map/ppermute | solution.py:548
  21.1 38.0 %collective-permute-start.6 = (bf16[24,2,32,384]{3,2,1,0:T(8,128)(2,1)}, bf16[24,2,32,384]{3,2,1,0:T(8,128)(2,1)}, u32[]{:S(2)}, u32[]{:S(2)}) collective-permute-start(bf16[24,2,32,384]{3,2,1,0:T(8,128)(2,1)} %get-tuple-element.40), channel_id=1, source_target_pairs={{0,1},{3,2},{4,5},{7,6},{8,9},{11,10},{12,13},{15,14},{16,17},{19,... | collective-permute-start | bytes 3538952 | tf_op jit(solution)/shard_map/ppermute | solution.py:548
  35.2 10.6 %collective-permute-start.4 = (bf16[8,3,32,384]{3,2,1,0:T(8,128)(2,1)}, bf16[8,3,32,384]{3,2,1,0:T(8,128)(2,1)}, u32[]{:S(2)}, u32[]{:S(2)}) collective-permute-start(bf16[8,3,32,384]{3,2,1,0:T(8,128)(2,1)} %collective-permute-done.refs_2_.rest_1_), channel_id=1, source_target_pairs={{1,2},{2,1},{5,6},{6,5},{9,10},{10,9},{13,14},{14,13},{17,18},{18,... | collective-permute-start | bytes 1769480 | tf_op jit(solution)/shard_map/ppermute | solution.py:548
  36.7 9.0 %collective-permute-start.5 = (bf16[8,3,32,384]{3,2,1,0:T(8,128)(2,1)}, bf16[8,3,32,384]{3,2,1,0:T(8,128)(2,1)}, u32[]{:S(2)}, u32[]{:S(2)}) collective-permute-start(bf16[8,3,32,384]{3,2,1,0:T(8,128)(2,1)} %collective-permute-done.2.refs_2_.rest_1_), channel_id=1, source_target_pairs={{1,2},{2,1},{5,6},{6,5},{9,10},{10,9},{13,14},{14,13},{17,18},{18,... | collective-permute-start | bytes 1769480 | tf_op jit(solution)/shard_map/ppermute | solution.py:548
  38.2 29.8 %collective-permute-start.3 = (bf16[8,6,32,384]{3,2,1,0:T(8,128)(2,1)}, bf16[8,6,32,384]{3,2,1,0:T(8,128)(2,1)}, u32[]{:S(2)}, u32[]{:S(2)}) collective-permute-start(bf16[8,6,32,384]{3,2,1,0:T(8,128)(2,1)} %collective-permute-done.1.refs_3_.rest_2_), channel_id=1, source_target_pairs={{1,0},{2,3},{5,4},{6,7},{9,8},{10,11},{13,12},{14,15},{17,16},{18,... | collective-permute-start | bytes 3538952 | tf_op jit(solution)/shard_map/ppermute | solution.py:548
  61.1 8.2 %collective-permute-start.7 = (bf16[16,2,32,384]{3,2,1,0:T(8,128)(2,1)}, bf16[16,2,32,384]{3,2,1,0:T(8,128)(2,1)}, u32[]{:S(2)}, u32[]{:S(2)}) collective-permute-start(bf16[16,2,32,384]{3,2,1,0:T(8,128)(2,1)} %pad_maximum_fusion.1), channel_id=1, source_target_pairs={{1,2},{2,1},{5,6},{6,5},{9,10},{10,9},{13,14},{14,13},{17,18},{18,... | collective-permute-start | bytes 2359304 | tf_op jit(solution)/shard_map/ppermute | solution.py:548
  62.9 22.4 %collective-permute-start.8 = (bf16[8,3,32,384]{3,2,1,0:T(8,128)(2,1)}, bf16[8,3,32,384]{3,2,1,0:T(8,128)(2,1)S(1)}, u32[]{:S(2)}, u32[]{:S(2)}) collective-permute-start(bf16[8,3,32,384]{3,2,1,0:T(8,128)(2,1)} %collective-permute-done.4.refs_3_.rest_4_), channel_id=1, source_target_pairs={{1,0},{2,3},{5,4},{6,7},{9,8},{10,11},{13,12},{14,15},{17,16},{18,... | collective-permute-start | bytes 1769480 | tf_op jit(solution)/shard_map/ppermute | solution.py:548
  68.0 31.5 %collective-permute-start.10 = (bf16[8,3,32,384]{3,2,1,0:T(8,128)(2,1)}, bf16[8,3,32,384]{3,2,1,0:T(8,128)(2,1)S(1)}, u32[]{:S(2)}, u32[]{:S(2)}) collective-permute-start(bf16[8,3,32,384]{3,2,1,0:T(8,128)(2,1)} %collective-permute-done.5.refs_3_.rest_4_), channel_id=1, source_target_pairs={{1,0},{2,3},{5,4},{6,7},{9,8},{10,11},{13,12},{14,15},{17,16},{18,... | collective-permute-start | bytes 1769480 | tf_op jit(solution)/shard_map/ppermute | solution.py:548
  81.0 18.5 %collective-permute-start.9 = (f32[16,128]{1,0:T(8,128)S(1)}, f32[16,128]{1,0:T(8,128)S(1)}, u32[]{:S(2)}, u32[]{:S(2)}) collective-permute-start(f32[16,128]{1,0:T(8,128)S(1)} %correlate.16), channel_id=1, source_target_pairs={{1,0},{2,3},{5,4},{6,7},{9,8},{10,11},{13,12},{14,15},{17,16},{18,... | collective-permute-start | bytes 24584 | tf_op jit(solution)/shard_map/ppermute | solution.py:548
  82.4 28.0 %copy-start.7 = (bf16[8,3,32,384]{3,2,1,0:T(8,128)(2,1)S(1)}, bf16[8,3,32,384]{3,2,1,0:T(8,128)(2,1)}, u32[]{:S(2)}) copy-start(bf16[8,3,32,384]{3,2,1,0:T(8,128)(2,1)} %copy-done.6) | copy-start | bytes 1769476
  100.8 1.2 collective-permute-start.11
  102.0 4.5 %collective-permute-start.14 = (f32[16,128]{1,0:T(8,128)S(1)}, f32[16,128]{1,0:T(8,128)S(1)}, u32[]{:S(2)}, u32[]{:S(2)}) collective-permute-start(f32[16,128]{1,0:T(8,128)S(1)} %add.74), channel_id=1, source_target_pairs={{0,24},{4,28},{8,16},{12,20},{16,8},{20,12},{24,0},{28,4},{1,25},{... | collective-permute-start | bytes 24584 | tf_op jit(solution)/shard_map/ppermute | solution.py:533
  104.5 3.7 %collective-permute-start.13 = (f32[16,128]{1,0:T(8,128)S(1)}, f32[16,128]{1,0:T(8,128)S(1)}, u32[]{:S(2)}, u32[]{:S(2)}) collective-permute-start(f32[16,128]{1,0:T(8,128)S(1)} %add.74), channel_id=1, source_target_pairs={{0,16},{4,20},{8,24},{12,28},{16,0},{20,4},{24,8},{28,12},{1,17},{... | collective-permute-start | bytes 24584 | tf_op jit(solution)/shard_map/ppermute | solution.py:533
  105.0 3.7 %collective-permute-start.12 = (f32[16,128]{1,0:T(8,128)S(1)}, f32[16,128]{1,0:T(8,128)S(1)}, u32[]{:S(2)}, u32[]{:S(2)}) collective-permute-start(f32[16,128]{1,0:T(8,128)S(1)} %add.74), channel_id=1, source_target_pairs={{0,8},{4,12},{8,0},{12,4},{16,24},{20,28},{24,16},{28,20},{1,9},{5... | collective-permute-start | bytes 24584 | tf_op jit(solution)/shard_map/ppermute | solution.py:533
  108.6 5.5 %collective-permute-start.15 = (f32[16,128]{1,0:T(8,128)S(1)}, f32[16,128]{1,0:T(8,128)S(1)}, u32[]{:S(2)}, u32[]{:S(2)}) collective-permute-start(f32[16,128]{1,0:T(8,128)S(1)} %add_add_fusion.tot_ref), channel_id=1, source_target_pairs={{0,1},{3,2},{4,5},{7,6},{8,9},{11,10},{12,13},{15,14},{16,17},{19,... | collective-permute-start | bytes 24584 | tf_op jit(solution)/shard_map/ppermute | solution.py:548
  117.2 11.1 %collective-permute-start.18 = (f16[8,2,32,384]{3,2,1,0:T(8,128)(2,1)S(1)}, f16[8,2,32,384]{3,2,1,0:T(8,128)(2,1)S(1)}, u32[]{:S(2)}, u32[]{:S(2)}) collective-permute-start(f16[8,2,32,384]{3,2,1,0:T(8,128)(2,1)S(1)} %multiply_convert_fusion), channel_id=1, source_target_pairs={{1,0},{2,3},{5,4},{6,7},{9,8},{10,11},{13,12},{14,15},{17,16},{18,... | collective-permute-start | bytes 1179656 | tf_op jit(solution)/shard_map/ppermute | solution.py:548
  118.5 12.8 %collective-permute-start.17 = (bf16[8,3,32,384]{3,2,1,0:T(8,128)(2,1)S(1)}, bf16[8,3,32,384]{3,2,1,0:T(8,128)(2,1)S(1)}, u32[]{:S(2)}, u32[]{:S(2)}) collective-permute-start(bf16[8,3,32,384]{3,2,1,0:T(8,128)(2,1)S(1)} %get-tuple-element.50), channel_id=1, source_target_pairs={{4,0},{8,4},{12,8},{16,12},{20,16},{24,20},{28,24},{5,1},{9,5},{13... | collective-permute-start | bytes 1769480 | tf_op jit(solution)/shard_map/ppermute | solution.py:637
  124.0 7.3 %collective-permute-start.16 = (bf16[8,3,32,384]{3,2,1,0:T(8,128)(2,1)S(1)}, bf16[8,3,32,384]{3,2,1,0:T(8,128)(2,1)S(1)}, u32[]{:S(2)}, u32[]{:S(2)}) collective-permute-start(bf16[8,3,32,384]{3,2,1,0:T(8,128)(2,1)S(1)} %get-tuple-element.55), channel_id=1, source_target_pairs={{0,4},{4,8},{8,12},{12,16},{16,20},{20,24},{24,28},{1,5},{5,9},{9,... | collective-permute-start | bytes 1769480 | tf_op jit(solution)/shard_map/ppermute | solution.py:641
  140.0 3.5 %collective-permute-start.19 = (f32[8,128]{1,0:T(8,128)S(1)}, f32[8,128]{1,0:T(8,128)S(1)}, u32[]{:S(2)}, u32[]{:S(2)}) collective-permute-start(f32[8,128]{1,0:T(8,128)S(1)} %get-tuple-element.57), channel_id=1, source_target_pairs={{0,4},{4,0},{8,12},{12,8},{16,20},{20,16},{24,28},{28,24},{1,5},{5... | collective-permute-start | bytes 12296 | tf_op jit(solution)/shard_map/ppermute | solution.py:533
  143.5 6.7 %collective-permute-start.22 = (f32[8,128]{1,0:T(8,128)S(1)}, f32[8,128]{1,0:T(8,128)S(1)}, u32[]{:S(2)}, u32[]{:S(2)}) collective-permute-start(f32[8,128]{1,0:T(8,128)S(1)} %add.78), channel_id=1, source_target_pairs={{0,24},{4,28},{8,16},{12,20},{16,8},{20,12},{24,0},{28,4},{1,25},{... | collective-permute-start | bytes 12296 | tf_op jit(solution)/shard_map/ppermute | solution.py:533
  147.4 3.6 %collective-permute-start.21 = (f32[8,128]{1,0:T(8,128)S(1)}, f32[8,128]{1,0:T(8,128)S(1)}, u32[]{:S(2)}, u32[]{:S(2)}) collective-permute-start(f32[8,128]{1,0:T(8,128)S(1)} %add.78), channel_id=1, source_target_pairs={{0,16},{4,20},{8,24},{12,28},{16,0},{20,4},{24,8},{28,12},{1,17},{... | collective-permute-start | bytes 12296 | tf_op jit(solution)/shard_map/ppermute | solution.py:533
  148.1 3.6 %collective-permute-start.20 = (f32[8,128]{1,0:T(8,128)S(1)}, f32[8,128]{1,0:T(8,128)S(1)}, u32[]{:S(2)}, u32[]{:S(2)}) collective-permute-start(f32[8,128]{1,0:T(8,128)S(1)} %add.78), channel_id=1, source_target_pairs={{0,8},{4,12},{8,0},{12,4},{16,24},{20,28},{24,16},{28,20},{1,9},{5... | collective-permute-start | bytes 12296 | tf_op jit(solution)/shard_map/ppermute | solution.py:533
  (11 other events, 118.2 us)

commit v2 on v1

--- a/solution.py
+++ b/solution.py
@@ -297,74 +297,86 @@
     return [held(o[0]) for o in flat], layout
 
 
-def direction_kernel(layout, edges, base, aliased, tot_ref, info_ref, s_ref, d_ref, *rest):
+def direction_kernel(layout, first, edges, base, aliased, *refs):
+    if first:
+        (tot_ref, info_ref, cap_ref), refs = refs[:3], refs[3:]
+    else:
+        (info_ref, w_ref, scale_ref), refs = refs[:3], refs[3:]
+    (s_ref, d_ref), rest = refs[:2], refs[2:]
     groups, rest = grouped(rest, layout)
     if not edges:
-        (lost_ref, cap_ref), rest = rest[:2], rest[2:]
+        lost_ref, rest = rest[0], rest[1:]
     n_ref, rest = rest[aliased], rest[aliased + 1 :]
     if edges:
-        side_ref, rr_ref, rest = rest[0], rest[1], rest[2:]
-    w_ref, scale_ref = rest
+        side_ref, rest = rest[0], rest[1:]
     i = pl.program_id(0)
     count = info_ref.shape[0]
 
-    @pl.when(i == 0)
-    def _():
-        product, beta = scalars(tot_ref, info_ref)
-        chosen = coefficients(tot_ref, count)
-        scale_ref[0] = jnp.broadcast_to(beta, scale_ref.shape[1:])
-        if edges:
-            rr_ref[...] = jnp.broadcast_to(product, rr_ref.shape)
-        else:
-            scale_ref[1] = jnp.broadcast_to(reach(chosen, cap_ref), scale_ref.shape[1:])
-            chosen = chosen * info_ref[:, 2:3]
-        widened(chosen, w_ref)
+    if first:
+        w_ref, scale_ref = rest
+
+        @pl.when(i == 0)
+        def _():
+            product, beta = scalars(tot_ref, info_ref)
+            chosen = coefficients(tot_ref, count)
+            for number, column in enumerate((beta, reach(chosen, cap_ref), product)):
+                scale_ref[number] = jnp.broadcast_to(column, scale_ref.shape[1:])
+            widened(chosen, w_ref)
 
     beta = scale_ref[0][:, 0:1][:, :, None]
     for y in range(0, s_ref.shape[2], TILE):
         part = slice(y, y + TILE)
-        new = s_ref[:, base - 3 + i, part, :] - combined(w_ref, groups, i, y)
-        new = new + beta * d_ref[:, base - 3 + i, part, :]
+        removed = combined(w_ref, groups, i, y)
+        if not edges:
+            removed = info_ref[:, 2:3][:, :, None] * removed
+            removed = removed + scale_ref[1][:, 0:1][:, :, None] * lost_ref[:, 0, part, :]
+        new = s_ref[:, base - 3 + i, part, :] - removed + beta * d_ref[:, base - 3 + i, part, :]
         if edges:
             side_ref[:, 0, part, :] = new.astype(BF16)
-        else:
-            new = new - scale_ref[1][:, 0:1][:, :, None] * lost_ref[:, 0, part, :]
         n_ref[:, base + i, part, :] = new
 
 
-def directions(tot, info, start, direction, slots, steps, base, so_far=None, lost=None, cap=None):
+def directions(scalings, info, start, direction, slots, steps, base, so_far=None, lost=None):
     shape = start.shape
-    edges = lost is None
+    first, edges = so_far is None, lost is None
     wide = (shape[0], shape[1] + 6) + tuple(shape[2:])
     part = (shape[0], steps) + tuple(shape[2:])
     flat, layout = laid_out(slots)
-    args = [tot, info, held(start), held(direction), *flat]
-    in_specs = [whole_spec(tot.shape), whole_spec(info.shape)] + [DIRECT] * (2 + len(flat))
+    if first:
+        tot, cap = scalings
+        args = [tot, info, cap]
+        in_specs = [whole_spec(a.shape) for a in args]
+    else:
+        args = [info, held(scalings[0]), held(scalings[1])]
+        in_specs = [whole_spec(info.shape), DIRECT, DIRECT]
+    args += [held(start), held(direction), *flat]
+    in_specs += [DIRECT] * (2 + len(flat))
     if not edges:
-        args += [lost, cap]
-        in_specs += [plane_spec(part, same_plane), whole_spec(cap.shape)]
+        args.append(lost)
+        in_specs.append(plane_spec(part, same_plane))
     aliases = {}
-    if so_far is not None:
+    if not first:
         aliases = {len(args): 0}
         args.append(held(so_far))
         in_specs.append(DIRECT)
-    out_specs = [DIRECT]
-    out_shape = [near(wide, F32)]
+    out_specs, out_shape = [DIRECT], [near(wide, F32)]
     if edges:
-        out_specs += [plane_spec(part, same_plane), whole_spec(info.shape)]
-        out_shape += [near(part, BF16), jax.ShapeDtypeStruct(info.shape, F32)]
+        out_specs.append(plane_spec(part, same_plane))
+        out_shape.append(near(part, BF16))
+    if first:
+        out_specs += [DIRECT, DIRECT]
+        out_shape += [
+            near((2 * shape[0] * TILE, len(slots) * layout[0][0][0] * TILE), BF16),
+            near((3, shape[0], 128), F32),
+        ]
     work = 3 if edges else 64
     return pl.pallas_call(
-        functools.partial(direction_kernel, layout, edges, base, len(aliases)),
+        functools.partial(direction_kernel, layout, first, edges, base, len(aliases)),
         grid=(steps,),
         in_specs=in_specs,
         out_specs=out_specs,
         out_shape=out_shape,
         input_output_aliases=aliases,
-        scratch_shapes=[
-            pltpu.VMEM((2 * shape[0] * TILE, len(slots) * layout[0][0][0] * TILE), BF16),
-            pltpu.VMEM((2, shape[0], 128), F32),
-        ],
         compiler_params=params(6),
         cost_estimate=pl.CostEstimate(
             flops=steps * 2 * 256 * 1024 * 384, bytes_accessed=work * MIB, transcendentals=0
@@ -413,7 +425,7 @@
 
 def image_kernel(
     planes, info_ref, low_ref, high_ref, v_ref, wide_in, r_ref, x_ref,
-    new_ref, image_ref, curve_ref, keep_ref, n_ref, r_near, x_near, ky, even, odd, total, sem,
+    new_ref, image_ref, curve_ref, keep_ref, n_ref, r_near, x_near, ky, kz, even, odd, total, sem,
 ):
     i = pl.program_id(0)
     count, _, rows, depth = n_ref.shape
@@ -421,16 +433,17 @@
     @pl.when(i == 0)
     def _():
         ky[...] = band_matrix(count * rows, rows)
+        kz[...] = band_matrix(depth, depth)
         total[...] = jnp.zeros_like(total)
         pltpu.make_async_copy(r_ref, r_near, sem.at[0]).start()
         pltpu.make_async_copy(x_ref, x_near, sem.at[1]).start()
         n_ref[:, 0:3] = low_ref[...].astype(F32)
         n_ref[:, planes + 3 : planes + 6] = high_ref[...].astype(F32)
 
-    lane = lax.broadcasted_iota(jnp.int32, (rows, depth), 1)
     for half, beside in enumerate((even, odd)):
         high, low = split(n_ref[:, 2 * i + half + 3].reshape(count * rows, depth))
-        beside[...] = (dot(ky[...], high) + dot(ky[...], low)).reshape(beside.shape)
+        sides = dot(ky[...], high) + dot(ky[...], low) + dot(high, kz[...]) + dot(low, kz[...])
+        beside[...] = sides.reshape(beside.shape)
     for half, beside in enumerate((even, odd)):
         plane = 2 * i + half + 3
         shifted = v_ref[half] - 1.5 * K0
@@ -438,10 +451,7 @@
             here = n_ref[c, plane]
             side = beside[c]
             for away in range(1, 4):
-                below = jnp.where(lane >= away, pltpu.roll(here, away, 1), 0.0)
-                above = jnp.where(lane < depth - away, pltpu.roll(here, depth - away, 1), 0.0)
-                pair = n_ref[c, plane - away] + n_ref[c, plane + away]
-                side = side + SIDE[away - 1] * (below + above + pair)
+                side = side + SIDE[away - 1] * (n_ref[c, plane - away] + n_ref[c, plane + away])
             image = SCALE * side + (shifted - info_ref[c : c + 1, 1:2]) * here
             new_ref[c, half] = here
             keep_ref[c, plane - 3] = here
@@ -479,6 +489,7 @@
         input_output_aliases={4: 4},
         scratch_shapes=[
             pltpu.VMEM((count * rows, count * rows), BF16),
+            pltpu.VMEM((depth, depth), BF16),
             pltpu.VMEM((count, rows, depth), F32),
             pltpu.VMEM((count, rows, depth), F32),
             pltpu.VMEM((count, depth), F32),
@@ -594,7 +605,8 @@
         tot = correlate([tot], [lhs], kinds, [pair, inner], (1, 2), where, 3)
 
     edge_last = [hop(after(edge_far[0], tot), OUTWARD), hop(after(edge_far[1], tot, edge_next), OUTWARD)]
-    both = hop(jnp.concatenate([mid, after(got, tot, *edge_far)[2 * count :]]), INNER)
+    both = jnp.concatenate([mid, after(got, tot, *edge_far)[2 * count :]])
+    both = hop(after(both, edge_next), INNER)
     mid_pair, mid_inner, mid_far = piece(got, bands, 2 * count // bands), piece(both, bands, 0), piece(both, bands, 1)
     mids = [mid, mid_pair, mid_inner, mid_far]
     for nearer, farther, where in zip(sides(edge_next), edge_far, places):
@@ -633,22 +645,22 @@
         for half, inner, nearer in zip(range(2), sides(edge_inner), sides(edge_next))
     ]
     other_tot = hop(tot, INWARD)
-    wide, low, product = directions(tot, info, start, direction, slots[0], 3, 3)
+    wide, low, *scalings = directions((tot, cap), info, start, direction, slots[0], 3, 3)
     from_right = lax.ppermute(low, "grid", downward)
     lost = removals(after(other_tot, low), cap, [[mid_pair], [mid], [mid_inner], [mid_far]], count)
     lost = (lost * jnp.float32(TOP)).astype(jnp.float16)
-    wide, high, _ = directions(after(tot, lost), info, start, direction, slots[1], 3, 8, wide)
+    wide, high = directions(scalings, after(info, lost), start, direction, slots[1], 3, 8, wide)
     from_left = lax.ppermute(high, "grid", upward)
     lost = hop(lost, OUTWARD).astype(F32) * jnp.float32(1.0 / TOP)
     (wide,) = directions(
-        tot, info, start, direction, [[m] for m in mids], 2, 6, wide, lost, cap
+        scalings, info, start, direction, [[m] for m in mids], 2, 6, wide, lost
     )
     new, image, curve, keep, _, residual, solution = images(
         info, from_left, wide, from_right, potential, residual, solution
     )
     curve = grid_sum(curve)
     new_solution, new_residual = finish(tot, info, curve, keep, image, residual, solution)
-    return new_solution, new_residual, new, product[:, 0]
+    return new_solution, new_residual, new, scalings[1][2, :, 0]
 
 
 def solution(mesh):

time: 156 us -> 152 us (0.974)
  Pallas kernels: 58 us -> 55.9 us
  transfers between devices with their start and end apart: 23 -> 23, of which waited for: 13 -> 12; matrix products, arithmetic and copies ran while one was open for 3% -> 3% of each run, Pallas kernels for 27% -> 27%
where the time goes in v2:
time: 152 us; the launch traced here: 151 us
  Pallas kernels  55.9 us (37%)
  waiting for transfers between devices  43.7 us (29%)
  starting transfers between devices  40.1 us (26%)
  local copies, waits for them, and re-layouts  7.61 us (5%)
  other arithmetic  2.49 us (2%)
    ppermute x13, waiting for transfers between devices, hop(): return lax.ppermute(value, 'band', pairs)  37 us
    pallas_call x9, Pallas kernels, correlate(): pl.pallas_call(functools.partial(corr_kernel, slots, offsets, steps, len(...  24.9 us
    ppermute x13, starting transfers between devices, hop(): return lax.ppermute(value, 'band', pairs)  24 us
    ppermute x8, starting transfers between devices, grid_sum(): lax.ppermute(x, 'grid', [(i, i ^ step) for i in range(size)])  11.6 us
    pallas_call x3, Pallas kernels, directions(): pl.pallas_call(functools.partial(direction_kernel, layout, first, edges,...  9.77 us
    pallas_call x1, Pallas kernels, prepare(): pl.pallas_call(functools.partial(prepare_kernel, planes), grid=(planes,),...  7.6 us
    pallas_call x1, Pallas kernels, images(): pl.pallas_call(functools.partial(image_kernel, planes), grid=(planes // 2...  7.52 us
    ppermute x8, waiting for transfers between devices, grid_sum(): lax.ppermute(x, 'grid', [(i, i ^ step) for i in range(size)])  6.73 us
  transfers between devices with their start and end apart: 23, of which 12 were waited for; matrix products, arithmetic and copies ran while one was open for 3% of the time, Pallas kernels for 27%

profile of v2, /device:TPU:0, one launch (start us, length us, event | category | flops | bytes accessed | tf_op | source)
XLA Modules:
  0.0 151.0 jit_solution(10952918814312527322)
XLA Ops:
  3.9 4.9 %collective-permute-start.2 = (bf16[8,3,32,384]{3,2,1,0:T(8,128)(2,1)S(1)}, bf16[8,3,32,384]{3,2,1,0:T(8,128)(2,1)}, u32[]{:S(2)}, u32[]{:S(2)}) collective-permute-start(bf16[8,3,32,384]{3,2,1,0:T(8,128)(2,1)S(1)} %get-tuple-element.70.refs_5_), channel_id=1, source_target_pairs={{0,1},{1,0},{2,3},{3,2},{4,5},{5,4},{6,7},{7,6},{8,9},{9,8},{10,11... | collective-permute-start | bytes 1769480 | tf_op jit(solution)/shard_map/ppermute | solution.py:559
  10.2 7.6 %prepare.1 = (f32[8,8,32,384]{3,2,1,0:T(8,128)S(1)}, f32[8,8,32,384]{3,2,1,0:T(8,128)S(1)}, bf16[16,8,32,384]{3,2,1,0:T(8,128)(2,1)S(1)}, bf16[24,2,32,384]{3,2,1,0:T(8,128)(2,1)}, f32[16,128]{1,0:T(8,128)S(1)}) custom-call(f32[8,8,32,384]{3,2,1,0:T(8,128)} %r_ref.3, f32[8,8,32,384]{3,2,1,0:T(8,128)} %d_ref.1, f32[8,32,384]{2,1,0:T(8,128)} %v_ref.3, ...), custom_call_target="tpu_custom_call" | custom-call | flops 1000000 | bytes 1048576 | tf_op jit(solution)/shard_map/prepare/pallas_call | solution.py:135
  21.1 4.9 %collective-permute-start.6 = (bf16[24,2,32,384]{3,2,1,0:T(8,128)(2,1)}, bf16[24,2,32,384]{3,2,1,0:T(8,128)(2,1)}, u32[]{:S(2)}, u32[]{:S(2)}) collective-permute-start(bf16[24,2,32,384]{3,2,1,0:T(8,128)(2,1)} %get-tuple-element.42), channel_id=1, source_target_pairs={{0,1},{3,2},{4,5},{7,6},{8,9},{11,10},{12,13},{15,14},{16,17},{19,... | collective-permute-start | bytes 3538952 | tf_op jit(solution)/shard_map/ppermute | solution.py:559
  26.0 4.4 %correlate.9.refs_0_ = f32[16,128]{1,0:T(8,128)S(1)} custom-call(f32[16,128]{1,0:T(8,128)S(1)} %get-tuple-element.37.refs_0_, bf16[16,8,32,384]{3,2,1,0:T(8,128)(2,1)S(1)} %get-tuple-element.38.refs_1_.refs_3_, bf16[8,8,32,384]{3,2,1,0:T(8,128)(2,1)} %refs_2_.1), custom_call_target="tpu_custom_call" | custom-call | flops 1000000 | bytes 1048576 | tf_op jit(solution)/shard_map/correlate/pallas_call | solution.py:214
  31.7 3.5 %collective-permute-done.refs_2_.refs_6_ = bf16[8,3,32,384]{3,2,1,0:T(8,128)(2,1)} collective-permute-done((bf16[8,3,32,384]{3,2,1,0:T(8,128)(2,1)S(1)}, bf16[8,3,32,384]{3,2,1,0:T(8,128)(2,1)}, u32[]{:S(2)}, u32[]{:S(2)}) %collective-permute-start) | collective-permute-done | bytes 589856 | tf_op jit(solution)/shard_map/ppermute | solution.py:559
  38.2 3.1 %correlate.10.refs_0_ = f32[16,128]{1,0:T(8,128)S(1)} custom-call(f32[16,128]{1,0:T(8,128)S(1)} %correlate.9.refs_0_, bf16[16,8,32,384]{3,2,1,0:T(8,128)(2,1)S(1)} %get-tuple-element.38.refs_1_.refs_3_, bf16[8,3,32,384]{3,2,1,0:T(8,128)(2,1)} %collective-permute-done.refs_2_.refs_6_, bf16[8,6,32,384]{3,2,1,0:T(8,128)(2,1)} %collective-permute-done.1.refs_3_.refs_7_), custom_call_target="tpu_custom_call" | custom-call | flops 1000000 | bytes 1048576 | tf_op jit(solution)/shard_map/correlate/pallas_call | solution.py:214
  41.3 3.1 %correlate.11.refs_0_ = f32[16,128]{1,0:T(8,128)S(1)} custom-call(f32[16,128]{1,0:T(8,128)S(1)} %correlate.10.refs_0_, bf16[16,8,32,384]{3,2,1,0:T(8,128)(2,1)S(1)} %get-tuple-element.38.refs_1_.refs_3_, bf16[8,3,32,384]{3,2,1,0:T(8,128)(2,1)} %collective-permute-done.2.refs_2_.refs_6_, bf16[8,6,32,384]{3,2,1,0:T(8,128)(2,1)} %collective-permute-done.1.refs_3_.refs_7_), custom_call_target="tpu_custom_call" | custom-call | flops 1000000 | bytes 1048576 | tf_op jit(solution)/shard_map/correlate/pallas_call | solution.py:214
  44.4 14.7 %collective-permute-done.6.refs_3_.refs_1_.refs_5_.rest_0_.refs_6_ = bf16[24,2,32,384]{3,2,1,0:T(8,128)(2,1)} collective-permute-done((bf16[24,2,32,384]{3,2,1,0:T(8,128)(2,1)}, bf16[24,2,32,384]{3,2,1,0:T(8,128)(2,1)}, u32[]{:S(2)}, u32[]{:S(2)}) %collective-permute-start.6) | collective-permute-done | bytes 1179680 | tf_op jit(solution)/shard_map/ppermute | solution.py:559
  66.7 3.1 %correlate.12.refs_0_ = f32[16,128]{1,0:T(8,128)S(1)} custom-call(f32[16,128]{1,0:T(8,128)S(1)} %correlate.11.refs_0_, bf16[16,8,32,384]{3,2,1,0:T(8,128)(2,1)S(1)} %get-tuple-element.38.refs_1_.refs_3_, bf16[8,6,32,384]{3,2,1,0:T(8,128)(2,1)} %collective-permute-done.3.refs_2_.refs_8_, bf16[8,3,32,384]{3,2,1,0:T(8,128)(2,1)} %collective-permute-done.4.refs_3_.refs_9_), custom_call_target="tpu_custom_call" | custom-call | flops 1000000 | bytes 1048576 | tf_op jit(solution)/shard_map/correlate/pallas_call | solution.py:214
  69.8 3.1 %correlate.13.refs_0_ = f32[16,128]{1,0:T(8,128)S(1)} custom-call(f32[16,128]{1,0:T(8,128)S(1)} %correlate.12.refs_0_, bf16[16,8,32,384]{3,2,1,0:T(8,128)(2,1)S(1)} %get-tuple-element.38.refs_1_.refs_3_, bf16[8,6,32,384]{3,2,1,0:T(8,128)(2,1)} %collective-permute-done.3.refs_2_.refs_8_, bf16[8,3,32,384]{3,2,1,0:T(8,128)(2,1)} %collective-permute-done.5.refs_3_.refs_9_), custom_call_target="tpu_custom_call" | custom-call | flops 1000000 | bytes 1048576 | tf_op jit(solution)/shard_map/correlate/pallas_call | solution.py:214
  73.0 2.7 %correlate.16 = f32[16,128]{1,0:T(8,128)S(1)} custom-call(f32[16,128]{1,0:T(8,128)S(1)} %broadcast_in_dim.74.refs_0_, bf16[24,2,32,384]{3,2,1,0:T(8,128)(2,1)} %collective-permute-done.6.refs_3_.refs_1_.refs_5_.rest_0_.refs_6_, bf16[8,2,32,384]{3,2,1,0:T(8,128)(2,1)S(1)} %slice.15.o_ref.refs_2_.rest_1_.refs_5_, ...), custom_call_target="tpu_custom_call" | custom-call | flops 1000000 | bytes 1048576 | tf_op jit(solution)/shard_map/correlate/pallas_call | solution.py:214
  75.7 2.7 %correlate.14.refs_0_ = f32[16,128]{1,0:T(8,128)S(1)} custom-call(f32[16,128]{1,0:T(8,128)S(1)} %correlate.13.refs_0_, bf16[16,8,32,384]{3,2,1,0:T(8,128)(2,1)S(1)} %get-tuple-element.38.refs_1_.refs_3_, bf16[8,2,32,384]{3,2,1,0:T(8,128)(2,1)S(1)} %slice.15.o_ref.refs_2_.rest_1_.refs_5_, ...), custom_call_target="tpu_custom_call" | custom-call | flops 1000000 | bytes 1048576 | tf_op jit(solution)/shard_map/correlate/pallas_call | solution.py:214
  79.8 7.9 %collective-permute-done.8.refs_2_.refs_10_ = bf16[8,3,32,384]{3,2,1,0:T(8,128)(2,1)S(1)} collective-permute-done((bf16[8,3,32,384]{3,2,1,0:T(8,128)(2,1)}, bf16[8,3,32,384]{3,2,1,0:T(8,128)(2,1)S(1)}, u32[]{:S(2)}, u32[]{:S(2)}) %collective-permute-start.8) | collective-permute-done | bytes 589856 | tf_op jit(solution)/shard_map/ppermute | solution.py:559
  89.0 8.5 %collective-permute-done.9.refs_1_ = f32[16,128]{1,0:T(8,128)S(1)} collective-permute-done((f32[16,128]{1,0:T(8,128)S(1)}, f32[16,128]{1,0:T(8,128)S(1)}, u32[]{:S(2)}, u32[]{:S(2)}) %collective-permute-start.9) | collective-permute-done | bytes 8224 | tf_op jit(solution)/shard_map/ppermute | solution.py:559
  100.1 2.5 %collective-permute-start.14 = (f32[16,128]{1,0:T(8,128)S(1)}, f32[16,128]{1,0:T(8,128)S(1)}, u32[]{:S(2)}, u32[]{:S(2)}) collective-permute-start(f32[16,128]{1,0:T(8,128)S(1)} %add.74), channel_id=1, source_target_pairs={{0,24},{4,28},{8,16},{12,20},{16,8},{20,12},{24,0},{28,4},{1,25},{... | collective-permute-start | bytes 24584 | tf_op jit(solution)/shard_map/ppermute | solution.py:544
  108.2 3.7 %directions.3 = (f32[8,14,32,384]{3,2,1,0:T(8,128)S(1)}, bf16[8,3,32,384]{3,2,1,0:T(8,128)(2,1)S(1)}, bf16[256,512]{1,0:T(8,128)(2,1)S(1)}, f32[3,8,128]{2,1,0:T(8,128)S(1)}) custom-call(f32[16,128]{1,0:T(8,128)S(1)} %add_add_fusion.refs_0_.tot_ref, f32[8,128]{1,0:T(8,128)S(1)} %select_select_fusion.refs_1_.refs_0_.info_ref, ...), custom_call_target="tpu_custom_call" | custom-call | flops 603979776 | bytes 3145728 | tf_op jit(solution)/shard_map/directions/pallas_call | solution.py:373
  111.9 3.1 %removals.1 = f32[8,2,32,384]{3,2,1,0:T(8,128)S(1)} custom-call(f32[16,128]{1,0:T(8,128)S(1)} %collective-permute-done.15.tot_ref, f32[16,128]{1,0:T(8,128)S(1)} %multiply_add_fusion.refs_2_.cap_ref, bf16[24,2,32,384]{3,2,1,0:T(8,128)(2,1)} %collective-permute-done.6.refs_3_.refs_1_.refs_5_.rest_0_.refs_6_, ...), custom_call_target="tpu_custom_call" | custom-call | flops 402653184 | bytes 4194304 | tf_op jit(solution)/shard_map/removals/pallas_call | solution.py:409
  117.6 3.4 %directions.4 = (f32[8,14,32,384]{3,2,1,0:T(8,128)S(1)}, bf16[8,3,32,384]{3,2,1,0:T(8,128)(2,1)S(1)}) custom-call(f32[8,128]{1,0:T(8,128)S(1)} %select_select_fusion.refs_1_.refs_0_.info_ref, bf16[256,512]{1,0:T(8,128)(2,1)S(1)} %get-tuple-element.57.refs_1_, f32[3,8,128]{2,1,0:T(8,128)S(1)} %get-tuple-element.58.refs_2_, ...), custom_call_target="tpu_custom_call", output_to_operand_aliasing={{0}: (11, {})} | custom-call | flops 603979776 | bytes 3145728 | tf_op jit(solution)/shard_map/directions/pallas_call | solution.py:373
  121.1 3.2 %collective-permute-start.16 = (bf16[8,3,32,384]{3,2,1,0:T(8,128)(2,1)S(1)}, bf16[8,3,32,384]{3,2,1,0:T(8,128)(2,1)S(1)}, u32[]{:S(2)}, u32[]{:S(2)}) collective-permute-start(bf16[8,3,32,384]{3,2,1,0:T(8,128)(2,1)S(1)} %get-tuple-element.60), channel_id=1, source_target_pairs={{0,4},{4,8},{8,12},{12,16},{16,20},{20,24},{24,28},{1,5},{5,9},{9,... | collective-permute-start | bytes 1769480 | tf_op jit(solution)/shard_map/ppermute | solution.py:653
  126.3 2.7 %directions.5.wide_in = f32[8,14,32,384]{3,2,1,0:T(8,128)S(1)} custom-call(f32[8,128]{1,0:T(8,128)S(1)} %select_select_fusion.refs_1_.refs_0_.info_ref, bf16[256,512]{1,0:T(8,128)(2,1)S(1)} %get-tuple-element.57.refs_1_, f32[3,8,128]{2,1,0:T(8,128)S(1)} %get-tuple-element.58.refs_2_, ...), custom_call_target="tpu_custom_call", output_to_operand_aliasing={{}: (10, {})} | custom-call | flops 402653184 | bytes 67108864 | tf_op jit(solution)/shard_map/directions/pallas_call | solution.py:373
  129.0 7.5 %images.1 = (f32[8,8,32,384]{3,2,1,0:T(8,128)}, f32[8,8,32,384]{3,2,1,0:T(8,128)S(1)}, f32[8,128]{1,0:T(8,128)S(1)}, f32[8,8,32,384]{3,2,1,0:T(8,128)S(1)}, f32[...) custom-call(f32[8,128]{1,0:T(8,128)S(1)} %select_select_fusion.refs_, ...), custom_call_target="tpu_custom_call", output_to_operand_aliasing={{4}: (4, {})} | custom-call | flops 4000000000 | bytes 25165824 | tf_op jit(solution)/shard_map/images/pallas_call | solution.py:472
  136.6 2.1 %collective-permute-start.19 = (f32[8,128]{1,0:T(8,128)S(1)}, f32[8,128]{1,0:T(8,128)S(1)}, u32[]{:S(2)}, u32[]{:S(2)}) collective-permute-start(f32[8,128]{1,0:T(8,128)S(1)} %get-tuple-element.62), channel_id=1, source_target_pairs={{0,4},{4,0},{8,12},{12,8},{16,20},{20,16},{24,28},{28,24},{1,5},{5... | collective-permute-start | bytes 12296 | tf_op jit(solution)/shard_map/ppermute | solution.py:544
  139.5 4.7 %collective-permute-start.22 = (f32[8,128]{1,0:T(8,128)S(1)}, f32[8,128]{1,0:T(8,128)S(1)}, u32[]{:S(2)}, u32[]{:S(2)}) collective-permute-start(f32[8,128]{1,0:T(8,128)S(1)} %add.78), channel_id=1, source_target_pairs={{0,24},{4,28},{8,16},{12,20},{16,8},{20,12},{24,0},{28,4},{1,25},{... | collective-permute-start | bytes 12296 | tf_op jit(solution)/shard_map/ppermute | solution.py:544
  147.8 3.1 %finish.1 = (f32[8,8,32,384]{3,2,1,0:T(8,128)}, f32[8,8,32,384]{3,2,1,0:T(8,128)}) custom-call(f32[16,128]{1,0:T(8,128)S(1)} %add_add_fusion.refs_0_.tot_ref, f32[8,128]{1,0:T(8,128)S(1)} %select_select_fusion.refs_1_.refs_0_.info_ref, f32[8,128]{1,0:T(8,128)S(1)} %add_add_fusion.1.curve_ref, f32[8,8,32,384]{3,2,1,0:T(8,128)S(1)} %get-tuple-element.63.n_ref, ...), custom_call_target="tpu_custom_call" | custom-call | tf_op jit(solution)/shard_map/finish/pallas_call | solution.py:521
  (87 shorter events, 39.7 us)
Async XLA Ops:
  2.2 28.2 %collective-permute-start.1 = (bf16[8,6,32,384]{3,2,1,0:T(8,128)(2,1)S(1)}, bf16[8,6,32,384]{3,2,1,0:T(8,128)(2,1)}, u32[]{:S(2)}, u32[]{:S(2)}) collective-permute-start(bf16[8,6,32,384]{3,2,1,0:T(8,128)(2,1)S(1)} %pad_maximum_fusion), channel_id=1, source_target_pairs={{1,2},{2,1},{5,6},{6,5},{9,10},{10,9},{13,14},{14,13},{17,18},{18,... | collective-permute-start | bytes 3538952 | tf_op jit(solution)/shard_map/ppermute | solution.py:559
  3.9 27.8 %collective-permute-start.2 = (bf16[8,3,32,384]{3,2,1,0:T(8,128)(2,1)S(1)}, bf16[8,3,32,384]{3,2,1,0:T(8,128)(2,1)}, u32[]{:S(2)}, u32[]{:S(2)}) collective-permute-start(bf16[8,3,32,384]{3,2,1,0:T(8,128)(2,1)S(1)} %get-tuple-element.70.refs_5_), channel_id=1, source_target_pairs={{0,1},{1,0},{2,3},{3,2},{4,5},{5,4},{6,7},{7,6},{8,9},{9,8},{10,11... | collective-permute-start | bytes 1769480 | tf_op jit(solution)/shard_map/ppermute | solution.py:559
  8.8 26.4 %collective-permute-start = (bf16[8,3,32,384]{3,2,1,0:T(8,128)(2,1)S(1)}, bf16[8,3,32,384]{3,2,1,0:T(8,128)(2,1)}, u32[]{:S(2)}, u32[]{:S(2)}) collective-permute-start(bf16[8,3,32,384]{3,2,1,0:T(8,128)(2,1)S(1)} %get-tuple-element.71.refs_5_), channel_id=1, source_target_pairs={{0,1},{1,0},{2,3},{3,2},{4,5},{5,4},{6,7},{7,6},{8,9},{9,8},{10,11... | collective-permute-start | bytes 1769480 | tf_op jit(solution)/shard_map/ppermute | solution.py:559
  21.1 38.0 %collective-permute-start.6 = (bf16[24,2,32,384]{3,2,1,0:T(8,128)(2,1)}, bf16[24,2,32,384]{3,2,1,0:T(8,128)(2,1)}, u32[]{:S(2)}, u32[]{:S(2)}) collective-permute-start(bf16[24,2,32,384]{3,2,1,0:T(8,128)(2,1)} %get-tuple-element.42), channel_id=1, source_target_pairs={{0,1},{3,2},{4,5},{7,6},{8,9},{11,10},{12,13},{15,14},{16,17},{19,... | collective-permute-start | bytes 3538952 | tf_op jit(solution)/shard_map/ppermute | solution.py:559
  30.4 31.2 %collective-permute-start.3 = (bf16[8,6,32,384]{3,2,1,0:T(8,128)(2,1)}, bf16[8,6,32,384]{3,2,1,0:T(8,128)(2,1)}, u32[]{:S(2)}, u32[]{:S(2)}) collective-permute-start(bf16[8,6,32,384]{3,2,1,0:T(8,128)(2,1)} %collective-permute-done.1.refs_3_.refs_7_), channel_id=1, source_target_pairs={{1,0},{2,3},{5,4},{6,7},{9,8},{10,11},{13,12},{14,15},{17,16},{18,... | collective-permute-start | bytes 3538952 | tf_op jit(solution)/shard_map/ppermute | solution.py:559
  35.2 9.2 %collective-permute-start.4 = (bf16[8,3,32,384]{3,2,1,0:T(8,128)(2,1)}, bf16[8,3,32,384]{3,2,1,0:T(8,128)(2,1)}, u32[]{:S(2)}, u32[]{:S(2)}) collective-permute-start(bf16[8,3,32,384]{3,2,1,0:T(8,128)(2,1)} %collective-permute-done.refs_2_.refs_6_), channel_id=1, source_target_pairs={{1,2},{2,1},{5,6},{6,5},{9,10},{10,9},{13,14},{14,13},{17,18},{18,... | collective-permute-start | bytes 1769480 | tf_op jit(solution)/shard_map/ppermute | solution.py:559
  36.7 7.7 %collective-permute-start.5 = (bf16[8,3,32,384]{3,2,1,0:T(8,128)(2,1)}, bf16[8,3,32,384]{3,2,1,0:T(8,128)(2,1)}, u32[]{:S(2)}, u32[]{:S(2)}) collective-permute-start(bf16[8,3,32,384]{3,2,1,0:T(8,128)(2,1)} %collective-permute-done.2.refs_2_.refs_6_), channel_id=1, source_target_pairs={{1,2},{2,1},{5,6},{6,5},{9,10},{10,9},{13,14},{14,13},{17,18},{18,... | collective-permute-start | bytes 1769480 | tf_op jit(solution)/shard_map/ppermute | solution.py:559
  61.6 11.4 %collective-permute-start.7 = (bf16[16,2,32,384]{3,2,1,0:T(8,128)(2,1)}, bf16[16,2,32,384]{3,2,1,0:T(8,128)(2,1)}, u32[]{:S(2)}, u32[]{:S(2)}) collective-permute-start(bf16[16,2,32,384]{3,2,1,0:T(8,128)(2,1)} %pad_maximum_fusion.1), channel_id=1, source_target_pairs={{1,2},{2,1},{5,6},{6,5},{9,10},{10,9},{13,14},{14,13},{17,18},{18,... | collective-permute-start | bytes 2359304 | tf_op jit(solution)/shard_map/ppermute | solution.py:559
  63.4 24.4 %collective-permute-start.8 = (bf16[8,3,32,384]{3,2,1,0:T(8,128)(2,1)}, bf16[8,3,32,384]{3,2,1,0:T(8,128)(2,1)S(1)}, u32[]{:S(2)}, u32[]{:S(2)}) collective-permute-start(bf16[8,3,32,384]{3,2,1,0:T(8,128)(2,1)} %collective-permute-done.4.refs_3_.refs_9_), channel_id=1, source_target_pairs={{1,0},{2,3},{5,4},{6,7},{9,8},{10,11},{13,12},{14,15},{17,16},{18,... | collective-permute-start | bytes 1769480 | tf_op jit(solution)/shard_map/ppermute | solution.py:559
  65.4 32.1 %collective-permute-start.10 = (bf16[8,3,32,384]{3,2,1,0:T(8,128)(2,1)}, bf16[8,3,32,384]{3,2,1,0:T(8,128)(2,1)S(1)}, u32[]{:S(2)}, u32[]{:S(2)}) collective-permute-start(bf16[8,3,32,384]{3,2,1,0:T(8,128)(2,1)} %collective-permute-done.5.refs_3_.refs_9_), channel_id=1, source_target_pairs={{1,0},{2,3},{5,4},{6,7},{9,8},{10,11},{13,12},{14,15},{17,16},{18,... | collective-permute-start | bytes 1769480 | tf_op jit(solution)/shard_map/ppermute | solution.py:559
  78.4 19.1 %collective-permute-start.9 = (f32[16,128]{1,0:T(8,128)S(1)}, f32[16,128]{1,0:T(8,128)S(1)}, u32[]{:S(2)}, u32[]{:S(2)}) collective-permute-start(f32[16,128]{1,0:T(8,128)S(1)} %correlate.16), channel_id=1, source_target_pairs={{1,0},{2,3},{5,4},{6,7},{9,8},{10,11},{13,12},{14,15},{17,16},{18,... | collective-permute-start | bytes 24584 | tf_op jit(solution)/shard_map/ppermute | solution.py:559
  79.8 28.4 %copy-start.7 = (bf16[8,3,32,384]{3,2,1,0:T(8,128)(2,1)S(1)}, bf16[8,3,32,384]{3,2,1,0:T(8,128)(2,1)}, u32[]{:S(2)}) copy-start(bf16[8,3,32,384]{3,2,1,0:T(8,128)(2,1)} %copy-done.6) | copy-start | bytes 1769476
  98.9 1.2 collective-permute-start.11
  100.1 4.5 %collective-permute-start.14 = (f32[16,128]{1,0:T(8,128)S(1)}, f32[16,128]{1,0:T(8,128)S(1)}, u32[]{:S(2)}, u32[]{:S(2)}) collective-permute-start(f32[16,128]{1,0:T(8,128)S(1)} %add.74), channel_id=1, source_target_pairs={{0,24},{4,28},{8,16},{12,20},{16,8},{20,12},{24,0},{28,4},{1,25},{... | collective-permute-start | bytes 24584 | tf_op jit(solution)/shard_map/ppermute | solution.py:544
  102.5 3.7 %collective-permute-start.13 = (f32[16,128]{1,0:T(8,128)S(1)}, f32[16,128]{1,0:T(8,128)S(1)}, u32[]{:S(2)}, u32[]{:S(2)}) collective-permute-start(f32[16,128]{1,0:T(8,128)S(1)} %add.74), channel_id=1, source_target_pairs={{0,16},{4,20},{8,24},{12,28},{16,0},{20,4},{24,8},{28,12},{1,17},{... | collective-permute-start | bytes 24584 | tf_op jit(solution)/shard_map/ppermute | solution.py:544
  103.0 3.7 %collective-permute-start.12 = (f32[16,128]{1,0:T(8,128)S(1)}, f32[16,128]{1,0:T(8,128)S(1)}, u32[]{:S(2)}, u32[]{:S(2)}) collective-permute-start(f32[16,128]{1,0:T(8,128)S(1)} %add.74), channel_id=1, source_target_pairs={{0,8},{4,12},{8,0},{12,4},{16,24},{20,28},{24,16},{28,20},{1,9},{5... | collective-permute-start | bytes 24584 | tf_op jit(solution)/shard_map/ppermute | solution.py:544
  106.7 5.2 %collective-permute-start.15 = (f32[16,128]{1,0:T(8,128)S(1)}, f32[16,128]{1,0:T(8,128)S(1)}, u32[]{:S(2)}, u32[]{:S(2)}) collective-permute-start(f32[16,128]{1,0:T(8,128)S(1)} %add_add_fusion.refs_0_.tot_ref), channel_id=1, source_target_pairs={{0,1},{3,2},{4,5},{7,6},{8,9},{11,10},{12,13},{15,14},{16,17},{19,... | collective-permute-start | bytes 24584 | tf_op jit(solution)/shard_map/ppermute | solution.py:559
  115.0 11.2 %collective-permute-start.18 = (f16[8,2,32,384]{3,2,1,0:T(8,128)(2,1)S(1)}, f16[8,2,32,384]{3,2,1,0:T(8,128)(2,1)S(1)}, u32[]{:S(2)}, u32[]{:S(2)}) collective-permute-start(f16[8,2,32,384]{3,2,1,0:T(8,128)(2,1)S(1)} %multiply_convert_fusion), channel_id=1, source_target_pairs={{1,0},{2,3},{5,4},{6,7},{9,8},{10,11},{13,12},{14,15},{17,16},{18,... | collective-permute-start | bytes 1179656 | tf_op jit(solution)/shard_map/ppermute | solution.py:559
  116.3 12.7 %collective-permute-start.17 = (bf16[8,3,32,384]{3,2,1,0:T(8,128)(2,1)S(1)}, bf16[8,3,32,384]{3,2,1,0:T(8,128)(2,1)S(1)}, u32[]{:S(2)}, u32[]{:S(2)}) collective-permute-start(bf16[8,3,32,384]{3,2,1,0:T(8,128)(2,1)S(1)} %get-tuple-element.54), channel_id=1, source_target_pairs={{4,0},{8,4},{12,8},{16,12},{20,16},{24,20},{28,24},{5,1},{9,5},{13... | collective-permute-start | bytes 1769480 | tf_op jit(solution)/shard_map/ppermute | solution.py:649
  121.1 8.0 %collective-permute-start.16 = (bf16[8,3,32,384]{3,2,1,0:T(8,128)(2,1)S(1)}, bf16[8,3,32,384]{3,2,1,0:T(8,128)(2,1)S(1)}, u32[]{:S(2)}, u32[]{:S(2)}) collective-permute-start(bf16[8,3,32,384]{3,2,1,0:T(8,128)(2,1)S(1)} %get-tuple-element.60), channel_id=1, source_target_pairs={{0,4},{4,8},{8,12},{12,16},{16,20},{20,24},{24,28},{1,5},{5,9},{9,... | collective-permute-start | bytes 1769480 | tf_op jit(solution)/shard_map/ppermute | solution.py:653
  136.6 2.9 %collective-permute-start.19 = (f32[8,128]{1,0:T(8,128)S(1)}, f32[8,128]{1,0:T(8,128)S(1)}, u32[]{:S(2)}, u32[]{:S(2)}) collective-permute-start(f32[8,128]{1,0:T(8,128)S(1)} %get-tuple-element.62), channel_id=1, source_target_pairs={{0,4},{4,0},{8,12},{12,8},{16,20},{20,16},{24,28},{28,24},{1,5},{5... | collective-permute-start | bytes 12296 | tf_op jit(solution)/shard_map/ppermute | solution.py:544
  139.5 6.7 %collective-permute-start.22 = (f32[8,128]{1,0:T(8,128)S(1)}, f32[8,128]{1,0:T(8,128)S(1)}, u32[]{:S(2)}, u32[]{:S(2)}) collective-permute-start(f32[8,128]{1,0:T(8,128)S(1)} %add.78), channel_id=1, source_target_pairs={{0,24},{4,28},{8,16},{12,20},{16,8},{20,12},{24,0},{28,4},{1,25},{... | collective-permute-start | bytes 12296 | tf_op jit(solution)/shard_map/ppermute | solution.py:544
  144.1 3.6 %collective-permute-start.21 = (f32[8,128]{1,0:T(8,128)S(1)}, f32[8,128]{1,0:T(8,128)S(1)}, u32[]{:S(2)}, u32[]{:S(2)}) collective-permute-start(f32[8,128]{1,0:T(8,128)S(1)} %add.78), channel_id=1, source_target_pairs={{0,16},{4,20},{8,24},{12,28},{16,0},{20,4},{24,8},{28,12},{1,17},{... | collective-permute-start | bytes 12296 | tf_op jit(solution)/shard_map/ppermute | solution.py:544
  144.1 3.6 %collective-permute-start.20 = (f32[8,128]{1,0:T(8,128)S(1)}, f32[8,128]{1,0:T(8,128)S(1)}, u32[]{:S(2)}, u32[]{:S(2)}) collective-permute-start(f32[8,128]{1,0:T(8,128)S(1)} %add.78), channel_id=1, source_target_pairs={{0,8},{4,12},{8,0},{12,4},{16,24},{20,28},{24,16},{28,20},{1,9},{5... | collective-permute-start | bytes 12296 | tf_op jit(solution)/shard_map/ppermute | solution.py:544
  (11 other events, 118.8 us)

commit v3 on v2

--- a/solution.py
+++ b/solution.py
@@ -391,25 +391,32 @@
     return jnp.maximum(jnp.sum(jnp.abs(chosen), axis=1, keepdims=True) * cap, 1e-30)
 
 
-def removal_kernel(layout, tot_ref, cap_ref, *rest):
+def removal_kernel(layout, flag_ref, tot_ref, cap_ref, *rest):
     groups, (out_ref, w_ref) = grouped(rest, layout)
 
-    @pl.when(pl.program_id(0) == 0)
+    @pl.when((pl.program_id(0) == 0) & (flag_ref[0] > 0))
     def _():
         chosen = coefficients(tot_ref, out_ref.shape[0])
         widened(chosen / reach(chosen, cap_ref), w_ref)
 
-    for y in range(0, out_ref.shape[2], TILE):
-        out_ref[:, 0, y : y + TILE, :] = combined(w_ref, groups, pl.program_id(0), y)
-
-
-def removals(tot, cap, slots, count):
+    @pl.when(flag_ref[0] > 0)
+    def _():
+        for y in range(0, out_ref.shape[2], TILE):
+            out_ref[:, 0, y : y + TILE, :] = combined(w_ref, groups, pl.program_id(0), y)
+
+    @pl.when(flag_ref[0] == 0)
+    def _():
+        out_ref[...] = jnp.zeros_like(out_ref)
+
+
+def removals(flag, tot, cap, slots, count):
     flat, layout = laid_out(slots)
     shape = (count,) + tuple(as_piece(slots[0][0])[1][1:])
     return pl.pallas_call(
         functools.partial(removal_kernel, layout),
         grid=(shape[1],),
-        in_specs=[whole_spec(tot.shape), whole_spec(cap.shape)] + [DIRECT] * len(flat),
+        in_specs=[pl.BlockSpec(memory_space=pltpu.SMEM), whole_spec(tot.shape), whole_spec(cap.shape)]
+        + [DIRECT] * len(flat),
         out_specs=plane_spec(shape, same_plane),
         out_shape=near(shape, F32),
         scratch_shapes=[
@@ -420,7 +427,7 @@
             flops=2 * 2 * 256 * 1024 * 384, bytes_accessed=4 * MIB, transcendentals=0
         ),
         name="removals",
-    )(tot, cap, *flat)
+    )(flag, tot, cap, *flat)
 
 
 def image_kernel(
@@ -617,7 +624,7 @@
     )
     tot = correlate([tot], [lhs], kinds, mids, (0, 1, 2, 3), mid_plane, 2)
     taken = hop(after(given, tot), OUTWARD)
-    tot = correlate([tot], [lhs], kinds, [edge_last[0]], (3,), same_plane, 3)
+    tot = correlate([tot], [lhs], kinds, [held(edge_last[0])], (3,), same_plane, 3)
 
     lane = lax.iota(jnp.int32, 128)
     group = jnp.where(
@@ -636,8 +643,9 @@
         jnp.where(lane[None, :] == 1, energy[:, None], inside),
     )
     cap = given * inside + taken
-    tot, cap, info, member = lax.optimization_barrier((tot, cap, info, member))
-    tot = correlate([tot, taken], [lhs], kinds, [edge_last[1]], (3,), high_plane, 3, False, member)
+    flag = jnp.where(is_end, 0, 1).astype(jnp.int32).reshape(1)
+    tot, cap, info, member, flag = lax.optimization_barrier((tot, cap, info, member, flag))
+    tot = correlate([tot, taken], [lhs], kinds, [held(edge_last[1])], (3,), high_plane, 3, False, member)
     tot = grid_sum(tot)
 
     slots = [
@@ -647,7 +655,7 @@
     other_tot = hop(tot, INWARD)
     wide, low, *scalings = directions((tot, cap), info, start, direction, slots[0], 3, 3)
     from_right = lax.ppermute(low, "grid", downward)
-    lost = removals(after(other_tot, low), cap, [[mid_pair], [mid], [mid_inner], [mid_far]], count)
+    lost = removals(flag, after(other_tot, low), cap, [[mid_pair], [mid], [mid_inner], [mid_far]], count)
     lost = (lost * jnp.float32(TOP)).astype(jnp.float16)
     wide, high = directions(scalings, after(info, lost), start, direction, slots[1], 3, 8, wide)
     from_left = lax.ppermute(high, "grid", upward)

time: 152 us -> 156 us (1.026)
  Pallas kernels: 55.9 us -> 58.9 us
  waiting for transfers between devices: 43.7 us -> 40.8 us
  starting transfers between devices: 40.1 us -> 42.1 us
    pallas_call x9, Pallas kernels: 24.9 us -> 28.4 us  [correlate(): pl.pallas_call(functools.partial(corr_kernel, slots, offsets, steps, len(...]
    ppermute x13, waiting for transfers between devices: 37 us -> 34.1 us  [hop(): return lax.ppermute(value, 'band', pairs)]
    ppermute x13, starting transfers between devices: 24 us -> 25.7 us  [hop(): return lax.ppermute(value, 'band', pairs)]
  transfers between devices with their start and end apart: 23 -> 23, of which waited for: 12 -> 13; matrix products, arithmetic and copies ran while one was open for 3% -> 5% of each run, Pallas kernels for 27% -> 28%
where the time goes in v3:
time: 156 us; the launch traced here: 155 us
  Pallas kernels  58.9 us (38%)
  starting transfers between devices  42.1 us (27%)
  waiting for transfers between devices  40.8 us (26%)
  local copies, waits for them, and re-layouts  8.12 us (5%)
  other arithmetic  3.86 us (2%)
    ppermute x13, waiting for transfers between devices, hop(): return lax.ppermute(value, 'band', pairs)  34.1 us
    pallas_call x9, Pallas kernels, correlate(): pl.pallas_call(functools.partial(corr_kernel, slots, offsets, steps, len(...  28.4 us
    ppermute x13, starting transfers between devices, hop(): return lax.ppermute(value, 'band', pairs)  25.7 us
    ppermute x8, starting transfers between devices, grid_sum(): lax.ppermute(x, 'grid', [(i, i ^ step) for i in range(size)])  11.9 us
    pallas_call x3, Pallas kernels, directions(): pl.pallas_call(functools.partial(direction_kernel, layout, first, edges,...  10.2 us
    pallas_call x1, Pallas kernels, images(): pl.pallas_call(functools.partial(image_kernel, planes), grid=(planes // 2...  7.75 us
    pallas_call x1, Pallas kernels, prepare(): pl.pallas_call(functools.partial(prepare_kernel, planes), grid=(planes,),...  7.6 us
    ppermute x8, waiting for transfers between devices, grid_sum(): lax.ppermute(x, 'grid', [(i, i ^ step) for i in range(size)])  6.64 us
  transfers between devices with their start and end apart: 23, of which 13 were waited for; matrix products, arithmetic and copies ran while one was open for 5% of the time, Pallas kernels for 28%

profile of v3, /device:TPU:0, one launch (start us, length us, event | category | flops | bytes accessed | tf_op | source)
XLA Modules:
  0.0 154.9 jit_solution(9662730807102726500)
XLA Ops:
  3.9 4.9 %collective-permute-start.2 = (bf16[8,3,32,384]{3,2,1,0:T(8,128)(2,1)S(1)}, bf16[8,3,32,384]{3,2,1,0:T(8,128)(2,1)}, u32[]{:S(2)}, u32[]{:S(2)}) collective-permute-start(bf16[8,3,32,384]{3,2,1,0:T(8,128)(2,1)S(1)} %get-tuple-element.72.refs_5_), channel_id=1, source_target_pairs={{0,1},{1,0},{2,3},{3,2},{4,5},{5,4},{6,7},{7,6},{8,9},{9,8},{10,11... | collective-permute-start | bytes 1769480 | tf_op jit(solution)/shard_map/ppermute | solution.py:566
  10.2 7.6 %prepare.1 = (f32[8,8,32,384]{3,2,1,0:T(8,128)S(1)}, f32[8,8,32,384]{3,2,1,0:T(8,128)S(1)}, bf16[16,8,32,384]{3,2,1,0:T(8,128)(2,1)S(1)}, bf16[24,2,32,384]{3,2,1,0:T(8,128)(2,1)}, f32[16,128]{1,0:T(8,128)S(1)}) custom-call(f32[8,8,32,384]{3,2,1,0:T(8,128)} %r_ref.3, f32[8,8,32,384]{3,2,1,0:T(8,128)} %d_ref.1, f32[8,32,384]{2,1,0:T(8,128)} %v_ref.3, ...), custom_call_target="tpu_custom_call" | custom-call | flops 1000000 | bytes 1048576 | tf_op jit(solution)/shard_map/prepare/pallas_call | solution.py:135
  21.1 4.9 %collective-permute-start.6 = (bf16[24,2,32,384]{3,2,1,0:T(8,128)(2,1)}, bf16[24,2,32,384]{3,2,1,0:T(8,128)(2,1)}, u32[]{:S(2)}, u32[]{:S(2)}) collective-permute-start(bf16[24,2,32,384]{3,2,1,0:T(8,128)(2,1)} %get-tuple-element.43), channel_id=1, source_target_pairs={{0,1},{3,2},{4,5},{7,6},{8,9},{11,10},{12,13},{15,14},{16,17},{19,... | collective-permute-start | bytes 3538952 | tf_op jit(solution)/shard_map/ppermute | solution.py:566
  26.0 4.4 %correlate.9.refs_0_ = f32[16,128]{1,0:T(8,128)S(1)} custom-call(f32[16,128]{1,0:T(8,128)S(1)} %get-tuple-element.38.refs_0_, bf16[16,8,32,384]{3,2,1,0:T(8,128)(2,1)S(1)} %get-tuple-element.39.refs_1_.refs_3_, bf16[8,8,32,384]{3,2,1,0:T(8,128)(2,1)} %refs_2_.1), custom_call_target="tpu_custom_call" | custom-call | flops 1000000 | bytes 1048576 | tf_op jit(solution)/shard_map/correlate/pallas_call | solution.py:214
  31.7 3.5 %collective-permute-done.refs_2_.refs_6_ = bf16[8,3,32,384]{3,2,1,0:T(8,128)(2,1)} collective-permute-done((bf16[8,3,32,384]{3,2,1,0:T(8,128)(2,1)S(1)}, bf16[8,3,32,384]{3,2,1,0:T(8,128)(2,1)}, u32[]{:S(2)}, u32[]{:S(2)}) %collective-permute-start) | collective-permute-done | bytes 589856 | tf_op jit(solution)/shard_map/ppermute | solution.py:566
  38.2 3.1 %correlate.10.refs_0_ = f32[16,128]{1,0:T(8,128)S(1)} custom-call(f32[16,128]{1,0:T(8,128)S(1)} %correlate.9.refs_0_, bf16[16,8,32,384]{3,2,1,0:T(8,128)(2,1)S(1)} %get-tuple-element.39.refs_1_.refs_3_, bf16[8,3,32,384]{3,2,1,0:T(8,128)(2,1)} %collective-permute-done.refs_2_.refs_6_, bf16[8,6,32,384]{3,2,1,0:T(8,128)(2,1)} %collective-permute-done.1.refs_3_.refs_7_), custom_call_target="tpu_custom_call" | custom-call | flops 1000000 | bytes 1048576 | tf_op jit(solution)/shard_map/correlate/pallas_call | solution.py:214
  41.3 3.1 %correlate.11.refs_0_ = f32[16,128]{1,0:T(8,128)S(1)} custom-call(f32[16,128]{1,0:T(8,128)S(1)} %correlate.10.refs_0_, bf16[16,8,32,384]{3,2,1,0:T(8,128)(2,1)S(1)} %get-tuple-element.39.refs_1_.refs_3_, bf16[8,3,32,384]{3,2,1,0:T(8,128)(2,1)} %collective-permute-done.2.refs_2_.refs_6_, bf16[8,6,32,384]{3,2,1,0:T(8,128)(2,1)} %collective-permute-done.1.refs_3_.refs_7_), custom_call_target="tpu_custom_call" | custom-call | flops 1000000 | bytes 1048576 | tf_op jit(solution)/shard_map/correlate/pallas_call | solution.py:214
  44.4 14.7 %collective-permute-done.6.refs_3_.refs_1_.refs_5_.rest_0_.refs_6_ = bf16[24,2,32,384]{3,2,1,0:T(8,128)(2,1)} collective-permute-done((bf16[24,2,32,384]{3,2,1,0:T(8,128)(2,1)}, bf16[24,2,32,384]{3,2,1,0:T(8,128)(2,1)}, u32[]{:S(2)}, u32[]{:S(2)}) %collective-permute-start.6) | collective-permute-done | bytes 1179680 | tf_op jit(solution)/shard_map/ppermute | solution.py:566
  67.9 3.1 %correlate.12.refs_0_ = f32[16,128]{1,0:T(8,128)S(1)} custom-call(f32[16,128]{1,0:T(8,128)S(1)} %correlate.11.refs_0_, bf16[16,8,32,384]{3,2,1,0:T(8,128)(2,1)S(1)} %get-tuple-element.39.refs_1_.refs_3_, bf16[8,6,32,384]{3,2,1,0:T(8,128)(2,1)} %collective-permute-done.3.refs_2_.refs_8_, bf16[8,3,32,384]{3,2,1,0:T(8,128)(2,1)} %collective-permute-done.4.refs_3_.refs_9_), custom_call_target="tpu_custom_call" | custom-call | flops 1000000 | bytes 1048576 | tf_op jit(solution)/shard_map/correlate/pallas_call | solution.py:214
  71.0 3.1 %correlate.13.refs_0_ = f32[16,128]{1,0:T(8,128)S(1)} custom-call(f32[16,128]{1,0:T(8,128)S(1)} %correlate.12.refs_0_, bf16[16,8,32,384]{3,2,1,0:T(8,128)(2,1)S(1)} %get-tuple-element.39.refs_1_.refs_3_, bf16[8,6,32,384]{3,2,1,0:T(8,128)(2,1)} %collective-permute-done.3.refs_2_.refs_8_, bf16[8,3,32,384]{3,2,1,0:T(8,128)(2,1)} %collective-permute-done.5.refs_3_.refs_9_), custom_call_target="tpu_custom_call" | custom-call | flops 1000000 | bytes 1048576 | tf_op jit(solution)/shard_map/correlate/pallas_call | solution.py:214
  74.2 3.3 %correlate.16 = f32[16,128]{1,0:T(8,128)} custom-call(f32[16,128]{1,0:T(8,128)S(1)} %broadcast_in_dim.74.refs_0_, bf16[24,2,32,384]{3,2,1,0:T(8,128)(2,1)} %collective-permute-done.6.refs_3_.refs_1_.refs_5_.rest_0_.refs_6_, bf16[8,2,32,384]{3,2,1,0:T(8,128)(2,1)S(1)} %slice.15.o_ref.refs_2_.rest_1_.refs_5_, ...), custom_call_target="tpu_custom_call" | custom-call | flops 1000000 | bytes 1048576 | tf_op jit(solution)/shard_map/correlate/pallas_call | solution.py:214
  77.5 2.7 %correlate.14.refs_0_ = f32[16,128]{1,0:T(8,128)S(1)} custom-call(f32[16,128]{1,0:T(8,128)S(1)} %correlate.13.refs_0_, bf16[16,8,32,384]{3,2,1,0:T(8,128)(2,1)S(1)} %get-tuple-element.39.refs_1_.refs_3_, bf16[8,2,32,384]{3,2,1,0:T(8,128)(2,1)S(1)} %slice.15.o_ref.refs_2_.rest_1_.refs_5_, ...), custom_call_target="tpu_custom_call" | custom-call | flops 1000000 | bytes 1048576 | tf_op jit(solution)/shard_map/correlate/pallas_call | solution.py:214
  81.6 6.8 %collective-permute-done.8.refs_2_.refs_10_ = bf16[8,3,32,384]{3,2,1,0:T(8,128)(2,1)} collective-permute-done((bf16[8,3,32,384]{3,2,1,0:T(8,128)(2,1)}, bf16[8,3,32,384]{3,2,1,0:T(8,128)(2,1)}, u32[]{:S(2)}, u32[]{:S(2)}) %collective-permute-start.8) | collective-permute-done | bytes 589856 | tf_op jit(solution)/shard_map/ppermute | solution.py:566
  88.4 2.8 %correlate.15.refs_0_ = f32[16,128]{1,0:T(8,128)S(1)} custom-call(f32[16,128]{1,0:T(8,128)S(1)} %correlate.14.refs_0_, bf16[16,8,32,384]{3,2,1,0:T(8,128)(2,1)S(1)} %get-tuple-element.39.refs_1_.refs_3_, bf16[8,3,32,384]{3,2,1,0:T(8,128)(2,1)} %collective-permute-done.8.refs_2_.refs_10_), custom_call_target="tpu_custom_call" | custom-call | flops 1000000 | bytes 1048576 | tf_op jit(solution)/shard_map/correlate/pallas_call | solution.py:214
  91.1 7.1 %collective-permute-done.9.refs_1_ = f32[16,128]{1,0:T(8,128)} collective-permute-done((f32[16,128]{1,0:T(8,128)}, f32[16,128]{1,0:T(8,128)}, u32[]{:S(2)}, u32[]{:S(2)}) %collective-permute-start.9) | collective-permute-done | bytes 8224 | tf_op jit(solution)/shard_map/ppermute | solution.py:566
  98.9 2.8 %correlate.17 = f32[16,128]{1,0:T(8,128)S(1)} custom-call(f32[16,128]{1,0:T(8,128)S(1)} %correlate.15.refs_0_, f32[16,128]{1,0:T(8,128)} %collective-permute-done.9.refs_1_, f32[8,128]{1,0:T(8,128)S(1)} %pad.4.refs_2_, bf16[16,8,32,384]{3,2,1,0:T(8,128)(2,1)S(1)} %get-tuple-element.39.refs_1_.refs_3_, ...), custom_call_target="tpu_custom_call" | custom-call | flops 1000000 | bytes 1048576 | tf_op jit(solution)/shard_map/correlate/pallas_call | solution.py:214
  109.5 3.2 %collective-permute-start.15 = (f32[16,128]{1,0:T(8,128)S(1)}, f32[16,128]{1,0:T(8,128)S(1)}, u32[]{:S(2)}, u32[]{:S(2)}) collective-permute-start(f32[16,128]{1,0:T(8,128)S(1)} %add_add_fusion.refs_0_.tot_ref), channel_id=1, source_target_pairs={{0,1},{3,2},{4,5},{7,6},{8,9},{11,10},{12,13},{15,14},{16,17},{19,... | collective-permute-start | bytes 24584 | tf_op jit(solution)/shard_map/ppermute | solution.py:566
  112.7 3.8 %directions.3 = (f32[8,14,32,384]{3,2,1,0:T(8,128)S(1)}, bf16[8,3,32,384]{3,2,1,0:T(8,128)(2,1)S(1)}, bf16[256,512]{1,0:T(8,128)(2,1)S(1)}, f32[3,8,128]{2,1,0:T(8,128)S(1)}) custom-call(f32[16,128]{1,0:T(8,128)S(1)} %add_add_fusion.refs_0_.tot_ref, f32[8,128]{1,0:T(8,128)S(1)} %select_select_fusion.refs_1_.refs_0_.info_ref, ...), custom_call_target="tpu_custom_call" | custom-call | flops 603979776 | bytes 3145728 | tf_op jit(solution)/shard_map/directions/pallas_call | solution.py:373
  121.2 3.6 %directions.4 = (f32[8,14,32,384]{3,2,1,0:T(8,128)S(1)}, bf16[8,3,32,384]{3,2,1,0:T(8,128)(2,1)S(1)}) custom-call(f32[8,128]{1,0:T(8,128)S(1)} %select_select_fusion.refs_1_.refs_0_.info_ref, bf16[256,512]{1,0:T(8,128)(2,1)S(1)} %get-tuple-element.59.refs_1_, f32[3,8,128]{2,1,0:T(8,128)S(1)} %get-tuple-element.60.refs_2_, ...), custom_call_target="tpu_custom_call", output_to_operand_aliasing={{0}: (11, {})} | custom-call | flops 603979776 | bytes 3145728 | tf_op jit(solution)/shard_map/directions/pallas_call | solution.py:373
  124.8 3.2 %collective-permute-start.16 = (bf16[8,3,32,384]{3,2,1,0:T(8,128)(2,1)S(1)}, bf16[8,3,32,384]{3,2,1,0:T(8,128)(2,1)S(1)}, u32[]{:S(2)}, u32[]{:S(2)}) collective-permute-start(bf16[8,3,32,384]{3,2,1,0:T(8,128)(2,1)S(1)} %get-tuple-element.62), channel_id=1, source_target_pairs={{0,4},{4,8},{8,12},{12,16},{16,20},{20,24},{24,28},{1,5},{5,9},{9,... | collective-permute-start | bytes 1769480 | tf_op jit(solution)/shard_map/ppermute | solution.py:661
  129.8 2.7 %directions.5.wide_in = f32[8,14,32,384]{3,2,1,0:T(8,128)S(1)} custom-call(f32[8,128]{1,0:T(8,128)S(1)} %select_select_fusion.refs_1_.refs_0_.info_ref, bf16[256,512]{1,0:T(8,128)(2,1)S(1)} %get-tuple-element.59.refs_1_, f32[3,8,128]{2,1,0:T(8,128)S(1)} %get-tuple-element.60.refs_2_, ...), custom_call_target="tpu_custom_call", output_to_operand_aliasing={{}: (10, {})} | custom-call | flops 402653184 | bytes 67108864 | tf_op jit(solution)/shard_map/directions/pallas_call | solution.py:373
  132.5 7.8 %images.1 = (f32[8,8,32,384]{3,2,1,0:T(8,128)}, f32[8,8,32,384]{3,2,1,0:T(8,128)S(1)}, f32[8,128]{1,0:T(8,128)S(1)}, f32[8,8,32,384]{3,2,1,0:T(8,128)S(1)}, f32[...) custom-call(f32[8,128]{1,0:T(8,128)S(1)} %select_select_fusion.refs_, ...), custom_call_target="tpu_custom_call", output_to_operand_aliasing={{4}: (4, {})} | custom-call | flops 4000000000 | bytes 25165824 | tf_op jit(solution)/shard_map/images/pallas_call | solution.py:479
  143.5 4.4 %collective-permute-start.22 = (f32[8,128]{1,0:T(8,128)S(1)}, f32[8,128]{1,0:T(8,128)S(1)}, u32[]{:S(2)}, u32[]{:S(2)}) collective-permute-start(f32[8,128]{1,0:T(8,128)S(1)} %add.78), channel_id=1, source_target_pairs={{0,24},{4,28},{8,16},{12,20},{16,8},{20,12},{24,0},{28,4},{1,25},{... | collective-permute-start | bytes 12296 | tf_op jit(solution)/shard_map/ppermute | solution.py:551
  151.7 3.1 %finish.1 = (f32[8,8,32,384]{3,2,1,0:T(8,128)}, f32[8,8,32,384]{3,2,1,0:T(8,128)}) custom-call(f32[16,128]{1,0:T(8,128)S(1)} %add_add_fusion.refs_0_.tot_ref, f32[8,128]{1,0:T(8,128)S(1)} %select_select_fusion.refs_1_.refs_0_.info_ref, f32[8,128]{1,0:T(8,128)S(1)} %add_add_fusion.1.curve_ref, f32[8,8,32,384]{3,2,1,0:T(8,128)S(1)} %get-tuple-element.65.n_ref, ...), custom_call_target="tpu_custom_call" | custom-call | tf_op jit(solution)/shard_map/finish/pallas_call | solution.py:528
  (87 shorter events, 44.2 us)
Async XLA Ops:
  2.2 28.2 %collective-permute-start.1 = (bf16[8,6,32,384]{3,2,1,0:T(8,128)(2,1)S(1)}, bf16[8,6,32,384]{3,2,1,0:T(8,128)(2,1)}, u32[]{:S(2)}, u32[]{:S(2)}) collective-permute-start(bf16[8,6,32,384]{3,2,1,0:T(8,128)(2,1)S(1)} %pad_maximum_fusion), channel_id=1, source_target_pairs={{1,2},{2,1},{5,6},{6,5},{9,10},{10,9},{13,14},{14,13},{17,18},{18,... | collective-permute-start | bytes 3538952 | tf_op jit(solution)/shard_map/ppermute | solution.py:566
  3.9 27.8 %collective-permute-start.2 = (bf16[8,3,32,384]{3,2,1,0:T(8,128)(2,1)S(1)}, bf16[8,3,32,384]{3,2,1,0:T(8,128)(2,1)}, u32[]{:S(2)}, u32[]{:S(2)}) collective-permute-start(bf16[8,3,32,384]{3,2,1,0:T(8,128)(2,1)S(1)} %get-tuple-element.72.refs_5_), channel_id=1, source_target_pairs={{0,1},{1,0},{2,3},{3,2},{4,5},{5,4},{6,7},{7,6},{8,9},{9,8},{10,11... | collective-permute-start | bytes 1769480 | tf_op jit(solution)/shard_map/ppermute | solution.py:566
  8.8 26.4 %collective-permute-start = (bf16[8,3,32,384]{3,2,1,0:T(8,128)(2,1)S(1)}, bf16[8,3,32,384]{3,2,1,0:T(8,128)(2,1)}, u32[]{:S(2)}, u32[]{:S(2)}) collective-permute-start(bf16[8,3,32,384]{3,2,1,0:T(8,128)(2,1)S(1)} %get-tuple-element.73.refs_5_), channel_id=1, source_target_pairs={{0,1},{1,0},{2,3},{3,2},{4,5},{5,4},{6,7},{7,6},{8,9},{9,8},{10,11... | collective-permute-start | bytes 1769480 | tf_op jit(solution)/shard_map/ppermute | solution.py:566
  21.1 38.0 %collective-permute-start.6 = (bf16[24,2,32,384]{3,2,1,0:T(8,128)(2,1)}, bf16[24,2,32,384]{3,2,1,0:T(8,128)(2,1)}, u32[]{:S(2)}, u32[]{:S(2)}) collective-permute-start(bf16[24,2,32,384]{3,2,1,0:T(8,128)(2,1)} %get-tuple-element.43), channel_id=1, source_target_pairs={{0,1},{3,2},{4,5},{7,6},{8,9},{11,10},{12,13},{15,14},{16,17},{19,... | collective-permute-start | bytes 3538952 | tf_op jit(solution)/shard_map/ppermute | solution.py:566
  30.4 31.2 %collective-permute-start.3 = (bf16[8,6,32,384]{3,2,1,0:T(8,128)(2,1)}, bf16[8,6,32,384]{3,2,1,0:T(8,128)(2,1)}, u32[]{:S(2)}, u32[]{:S(2)}) collective-permute-start(bf16[8,6,32,384]{3,2,1,0:T(8,128)(2,1)} %collective-permute-done.1.refs_3_.refs_7_), channel_id=1, source_target_pairs={{1,0},{2,3},{5,4},{6,7},{9,8},{10,11},{13,12},{14,15},{17,16},{18,... | collective-permute-start | bytes 3538952 | tf_op jit(solution)/shard_map/ppermute | solution.py:566
  35.2 9.2 %collective-permute-start.4 = (bf16[8,3,32,384]{3,2,1,0:T(8,128)(2,1)}, bf16[8,3,32,384]{3,2,1,0:T(8,128)(2,1)}, u32[]{:S(2)}, u32[]{:S(2)}) collective-permute-start(bf16[8,3,32,384]{3,2,1,0:T(8,128)(2,1)} %collective-permute-done.refs_2_.refs_6_), channel_id=1, source_target_pairs={{1,2},{2,1},{5,6},{6,5},{9,10},{10,9},{13,14},{14,13},{17,18},{18,... | collective-permute-start | bytes 1769480 | tf_op jit(solution)/shard_map/ppermute | solution.py:566
  36.7 7.7 %collective-permute-start.5 = (bf16[8,3,32,384]{3,2,1,0:T(8,128)(2,1)}, bf16[8,3,32,384]{3,2,1,0:T(8,128)(2,1)}, u32[]{:S(2)}, u32[]{:S(2)}) collective-permute-start(bf16[8,3,32,384]{3,2,1,0:T(8,128)(2,1)} %collective-permute-done.2.refs_2_.refs_6_), channel_id=1, source_target_pairs={{1,2},{2,1},{5,6},{6,5},{9,10},{10,9},{13,14},{14,13},{17,18},{18,... | collective-permute-start | bytes 1769480 | tf_op jit(solution)/shard_map/ppermute | solution.py:566
  61.6 12.5 %collective-permute-start.7 = (bf16[16,2,32,384]{3,2,1,0:T(8,128)(2,1)}, bf16[16,2,32,384]{3,2,1,0:T(8,128)(2,1)}, u32[]{:S(2)}, u32[]{:S(2)}) collective-permute-start(bf16[16,2,32,384]{3,2,1,0:T(8,128)(2,1)} %pad_maximum_fusion.1), channel_id=1, source_target_pairs={{1,2},{2,1},{5,6},{6,5},{9,10},{10,9},{13,14},{14,13},{17,18},{18,... | collective-permute-start | bytes 2359304 | tf_op jit(solution)/shard_map/ppermute | solution.py:566
  63.9 24.5 %collective-permute-start.8 = (bf16[8,3,32,384]{3,2,1,0:T(8,128)(2,1)}, bf16[8,3,32,384]{3,2,1,0:T(8,128)(2,1)}, u32[]{:S(2)}, u32[]{:S(2)}) collective-permute-start(bf16[8,3,32,384]{3,2,1,0:T(8,128)(2,1)} %collective-permute-done.4.refs_3_.refs_9_), channel_id=1, source_target_pairs={{1,0},{2,3},{5,4},{6,7},{9,8},{10,11},{13,12},{14,15},{17,16},{18,... | collective-permute-start | bytes 1769480 | tf_op jit(solution)/shard_map/ppermute | solution.py:566
  65.9 33.0 %collective-permute-start.10 = (bf16[8,3,32,384]{3,2,1,0:T(8,128)(2,1)}, bf16[8,3,32,384]{3,2,1,0:T(8,128)(2,1)}, u32[]{:S(2)}, u32[]{:S(2)}) collective-permute-start(bf16[8,3,32,384]{3,2,1,0:T(8,128)(2,1)} %collective-permute-done.5.refs_3_.refs_9_), channel_id=1, source_target_pairs={{1,0},{2,3},{5,4},{6,7},{9,8},{10,11},{13,12},{14,15},{17,16},{18,... | collective-permute-start | bytes 1769480 | tf_op jit(solution)/shard_map/ppermute | solution.py:566
  80.2 18.0 %collective-permute-start.9 = (f32[16,128]{1,0:T(8,128)}, f32[16,128]{1,0:T(8,128)}, u32[]{:S(2)}, u32[]{:S(2)}) collective-permute-start(f32[16,128]{1,0:T(8,128)} %correlate.16), channel_id=1, source_target_pairs={{1,0},{2,3},{5,4},{6,7},{9,8},{10,11},{13,12},{14,15},{17,16},{18,... | collective-permute-start | bytes 24584 | tf_op jit(solution)/shard_map/ppermute | solution.py:566
  81.6 31.1 %copy-start.7 = (bf16[8,3,32,384]{3,2,1,0:T(8,128)(2,1)S(1)}, bf16[8,3,32,384]{3,2,1,0:T(8,128)(2,1)}, u32[]{:S(2)}) copy-start(bf16[8,3,32,384]{3,2,1,0:T(8,128)(2,1)} %copy-done.6) | copy-start | bytes 1769476
  101.7 1.2 collective-permute-start.11
  102.9 4.5 %collective-permute-start.14 = (f32[16,128]{1,0:T(8,128)S(1)}, f32[16,128]{1,0:T(8,128)S(1)}, u32[]{:S(2)}, u32[]{:S(2)}) collective-permute-start(f32[16,128]{1,0:T(8,128)S(1)} %add.74), channel_id=1, source_target_pairs={{0,24},{4,28},{8,16},{12,20},{16,8},{20,12},{24,0},{28,4},{1,25},{... | collective-permute-start | bytes 24584 | tf_op jit(solution)/shard_map/ppermute | solution.py:551
  105.3 3.7 %collective-permute-start.13 = (f32[16,128]{1,0:T(8,128)S(1)}, f32[16,128]{1,0:T(8,128)S(1)}, u32[]{:S(2)}, u32[]{:S(2)}) collective-permute-start(f32[16,128]{1,0:T(8,128)S(1)} %add.74), channel_id=1, source_target_pairs={{0,16},{4,20},{8,24},{12,28},{16,0},{20,4},{24,8},{28,12},{1,17},{... | collective-permute-start | bytes 24584 | tf_op jit(solution)/shard_map/ppermute | solution.py:551
  105.8 3.7 %collective-permute-start.12 = (f32[16,128]{1,0:T(8,128)S(1)}, f32[16,128]{1,0:T(8,128)S(1)}, u32[]{:S(2)}, u32[]{:S(2)}) collective-permute-start(f32[16,128]{1,0:T(8,128)S(1)} %add.74), channel_id=1, source_target_pairs={{0,8},{4,12},{8,0},{12,4},{16,24},{20,28},{24,16},{28,20},{1,9},{5... | collective-permute-start | bytes 24584 | tf_op jit(solution)/shard_map/ppermute | solution.py:551
  109.5 7.0 %collective-permute-start.15 = (f32[16,128]{1,0:T(8,128)S(1)}, f32[16,128]{1,0:T(8,128)S(1)}, u32[]{:S(2)}, u32[]{:S(2)}) collective-permute-start(f32[16,128]{1,0:T(8,128)S(1)} %add_add_fusion.refs_0_.tot_ref), channel_id=1, source_target_pairs={{0,1},{3,2},{4,5},{7,6},{8,9},{11,10},{12,13},{15,14},{16,17},{19,... | collective-permute-start | bytes 24584 | tf_op jit(solution)/shard_map/ppermute | solution.py:566
  118.6 11.1 %collective-permute-start.18 = (f16[8,2,32,384]{3,2,1,0:T(8,128)(2,1)S(1)}, f16[8,2,32,384]{3,2,1,0:T(8,128)(2,1)S(1)}, u32[]{:S(2)}, u32[]{:S(2)}) collective-permute-start(f16[8,2,32,384]{3,2,1,0:T(8,128)(2,1)S(1)} %multiply_convert_fusion), channel_id=1, source_target_pairs={{1,0},{2,3},{5,4},{6,7},{9,8},{10,11},{13,12},{14,15},{17,16},{18,... | collective-permute-start | bytes 1179656 | tf_op jit(solution)/shard_map/ppermute | solution.py:566
  119.9 12.6 %collective-permute-start.17 = (bf16[8,3,32,384]{3,2,1,0:T(8,128)(2,1)S(1)}, bf16[8,3,32,384]{3,2,1,0:T(8,128)(2,1)S(1)}, u32[]{:S(2)}, u32[]{:S(2)}) collective-permute-start(bf16[8,3,32,384]{3,2,1,0:T(8,128)(2,1)S(1)} %get-tuple-element.56), channel_id=1, source_target_pairs={{4,0},{8,4},{12,8},{16,12},{20,16},{24,20},{28,24},{5,1},{9,5},{13... | collective-permute-start | bytes 1769480 | tf_op jit(solution)/shard_map/ppermute | solution.py:657
  124.8 7.7 %collective-permute-start.16 = (bf16[8,3,32,384]{3,2,1,0:T(8,128)(2,1)S(1)}, bf16[8,3,32,384]{3,2,1,0:T(8,128)(2,1)S(1)}, u32[]{:S(2)}, u32[]{:S(2)}) collective-permute-start(bf16[8,3,32,384]{3,2,1,0:T(8,128)(2,1)S(1)} %get-tuple-element.62), channel_id=1, source_target_pairs={{0,4},{4,8},{8,12},{12,16},{16,20},{20,24},{24,28},{1,5},{5,9},{9,... | collective-permute-start | bytes 1769480 | tf_op jit(solution)/shard_map/ppermute | solution.py:661
  140.3 3.2 %collective-permute-start.19 = (f32[8,128]{1,0:T(8,128)S(1)}, f32[8,128]{1,0:T(8,128)S(1)}, u32[]{:S(2)}, u32[]{:S(2)}) collective-permute-start(f32[8,128]{1,0:T(8,128)S(1)} %get-tuple-element.64), channel_id=1, source_target_pairs={{0,4},{4,0},{8,12},{12,8},{16,20},{20,16},{24,28},{28,24},{1,5},{5... | collective-permute-start | bytes 12296 | tf_op jit(solution)/shard_map/ppermute | solution.py:551
  143.5 6.6 %collective-permute-start.22 = (f32[8,128]{1,0:T(8,128)S(1)}, f32[8,128]{1,0:T(8,128)S(1)}, u32[]{:S(2)}, u32[]{:S(2)}) collective-permute-start(f32[8,128]{1,0:T(8,128)S(1)} %add.78), channel_id=1, source_target_pairs={{0,24},{4,28},{8,16},{12,20},{16,8},{20,12},{24,0},{28,4},{1,25},{... | collective-permute-start | bytes 12296 | tf_op jit(solution)/shard_map/ppermute | solution.py:551
  147.9 3.6 %collective-permute-start.21 = (f32[8,128]{1,0:T(8,128)S(1)}, f32[8,128]{1,0:T(8,128)S(1)}, u32[]{:S(2)}, u32[]{:S(2)}) collective-permute-start(f32[8,128]{1,0:T(8,128)S(1)} %add.78), channel_id=1, source_target_pairs={{0,16},{4,20},{8,24},{12,28},{16,0},{20,4},{24,8},{28,12},{1,17},{... | collective-permute-start | bytes 12296 | tf_op jit(solution)/shard_map/ppermute | solution.py:551
  148.0 3.6 %collective-permute-start.20 = (f32[8,128]{1,0:T(8,128)S(1)}, f32[8,128]{1,0:T(8,128)S(1)}, u32[]{:S(2)}, u32[]{:S(2)}) collective-permute-start(f32[8,128]{1,0:T(8,128)S(1)} %add.78), channel_id=1, source_target_pairs={{0,8},{4,12},{8,0},{12,4},{16,24},{20,28},{24,16},{28,20},{1,9},{5... | collective-permute-start | bytes 12296 | tf_op jit(solution)/shard_map/ppermute | solution.py:551
  (11 other events, 123.3 us)

commit v4 on v2

--- a/solution.py
+++ b/solution.py
@@ -391,25 +391,29 @@
     return jnp.maximum(jnp.sum(jnp.abs(chosen), axis=1, keepdims=True) * cap, 1e-30)
 
 
-def removal_kernel(layout, tot_ref, cap_ref, *rest):
+def removal_kernel(layout, info_ref, tot_ref, cap_ref, *rest):
     groups, (out_ref, w_ref) = grouped(rest, layout)
-
-    @pl.when(pl.program_id(0) == 0)
+    inside = jnp.max(info_ref[:, 2:3]) > 0.0
+
+    @pl.when((pl.program_id(0) == 0) & inside)
     def _():
         chosen = coefficients(tot_ref, out_ref.shape[0])
         widened(chosen / reach(chosen, cap_ref), w_ref)
 
-    for y in range(0, out_ref.shape[2], TILE):
-        out_ref[:, 0, y : y + TILE, :] = combined(w_ref, groups, pl.program_id(0), y)
-
-
-def removals(tot, cap, slots, count):
+    @pl.when(inside)
+    def _():
+        for y in range(0, out_ref.shape[2], TILE):
+            out_ref[:, 0, y : y + TILE, :] = combined(w_ref, groups, pl.program_id(0), y)
+
+
+def removals(info, tot, cap, slots, count):
     flat, layout = laid_out(slots)
     shape = (count,) + tuple(as_piece(slots[0][0])[1][1:])
     return pl.pallas_call(
         functools.partial(removal_kernel, layout),
         grid=(shape[1],),
-        in_specs=[whole_spec(tot.shape), whole_spec(cap.shape)] + [DIRECT] * len(flat),
+        in_specs=[whole_spec(info.shape), whole_spec(tot.shape), whole_spec(cap.shape)]
+        + [DIRECT] * len(flat),
         out_specs=plane_spec(shape, same_plane),
         out_shape=near(shape, F32),
         scratch_shapes=[
@@ -420,7 +424,7 @@
             flops=2 * 2 * 256 * 1024 * 384, bytes_accessed=4 * MIB, transcendentals=0
         ),
         name="removals",
-    )(tot, cap, *flat)
+    )(info, tot, cap, *flat)
 
 
 def image_kernel(
@@ -647,7 +651,7 @@
     other_tot = hop(tot, INWARD)
     wide, low, *scalings = directions((tot, cap), info, start, direction, slots[0], 3, 3)
     from_right = lax.ppermute(low, "grid", downward)
-    lost = removals(after(other_tot, low), cap, [[mid_pair], [mid], [mid_inner], [mid_far]], count)
+    lost = removals(info, after(other_tot, low), cap, [[mid_pair], [mid], [mid_inner], [mid_far]], count)
     lost = (lost * jnp.float32(TOP)).astype(jnp.float16)
     wide, high = directions(scalings, after(info, lost), start, direction, slots[1], 3, 8, wide)
     from_left = lax.ppermute(high, "grid", upward)

time: 152 us -> 151 us (level)
  no operation moved by 1% of the time
where the time goes in v4:
time: 151 us; the launch traced here: 150 us
  Pallas kernels  55 us (36%)
  waiting for transfers between devices  43.7 us (29%)
  starting transfers between devices  40.1 us (27%)
  local copies, waits for them, and re-layouts  7.61 us (5%)
  other arithmetic  2.49 us (2%)
    ppermute x13, waiting for transfers between devices, hop(): return lax.ppermute(value, 'band', pairs)  37 us
    pallas_call x9, Pallas kernels, correlate(): pl.pallas_call(functools.partial(corr_kernel, slots, offsets, steps, len(...  24.9 us
    ppermute x13, starting transfers between devices, hop(): return lax.ppermute(value, 'band', pairs)  24 us
    ppermute x8, starting transfers between devices, grid_sum(): lax.ppermute(x, 'grid', [(i, i ^ step) for i in range(size)])  11.6 us
    pallas_call x3, Pallas kernels, directions(): pl.pallas_call(functools.partial(direction_kernel, layout, first, edges,...  9.77 us
    pallas_call x1, Pallas kernels, prepare(): pl.pallas_call(functools.partial(prepare_kernel, planes), grid=(planes,),...  7.6 us
    pallas_call x1, Pallas kernels, images(): pl.pallas_call(functools.partial(image_kernel, planes), grid=(planes // 2...  7.51 us
    ppermute x8, waiting for transfers between devices, grid_sum(): lax.ppermute(x, 'grid', [(i, i ^ step) for i in range(size)])  6.73 us
  transfers between devices with their start and end apart: 23, of which 12 were waited for; matrix products, arithmetic and copies ran while one was open for 3% of the time, Pallas kernels for 27%

profile of v4, /device:TPU:0, one launch (start us, length us, event | category | flops | bytes accessed | tf_op | source)
XLA Modules:
  0.0 150.1 jit_solution(8772097191551663769)
XLA Ops:
  3.9 4.9 %collective-permute-start.2 = (bf16[8,3,32,384]{3,2,1,0:T(8,128)(2,1)S(1)}, bf16[8,3,32,384]{3,2,1,0:T(8,128)(2,1)}, u32[]{:S(2)}, u32[]{:S(2)}) collective-permute-start(bf16[8,3,32,384]{3,2,1,0:T(8,128)(2,1)S(1)} %get-tuple-element.70.refs_5_), channel_id=1, source_target_pairs={{0,1},{1,0},{2,3},{3,2},{4,5},{5,4},{6,7},{7,6},{8,9},{9,8},{10,11... | collective-permute-start | bytes 1769480 | tf_op jit(solution)/shard_map/ppermute | solution.py:563
  10.2 7.6 %prepare.1 = (f32[8,8,32,384]{3,2,1,0:T(8,128)S(1)}, f32[8,8,32,384]{3,2,1,0:T(8,128)S(1)}, bf16[16,8,32,384]{3,2,1,0:T(8,128)(2,1)S(1)}, bf16[24,2,32,384]{3,2,1,0:T(8,128)(2,1)}, f32[16,128]{1,0:T(8,128)S(1)}) custom-call(f32[8,8,32,384]{3,2,1,0:T(8,128)} %r_ref.3, f32[8,8,32,384]{3,2,1,0:T(8,128)} %d_ref.1, f32[8,32,384]{2,1,0:T(8,128)} %v_ref.3, ...), custom_call_target="tpu_custom_call" | custom-call | flops 1000000 | bytes 1048576 | tf_op jit(solution)/shard_map/prepare/pallas_call | solution.py:135
  21.1 4.9 %collective-permute-start.6 = (bf16[24,2,32,384]{3,2,1,0:T(8,128)(2,1)}, bf16[24,2,32,384]{3,2,1,0:T(8,128)(2,1)}, u32[]{:S(2)}, u32[]{:S(2)}) collective-permute-start(bf16[24,2,32,384]{3,2,1,0:T(8,128)(2,1)} %get-tuple-element.42), channel_id=1, source_target_pairs={{0,1},{3,2},{4,5},{7,6},{8,9},{11,10},{12,13},{15,14},{16,17},{19,... | collective-permute-start | bytes 3538952 | tf_op jit(solution)/shard_map/ppermute | solution.py:563
  26.0 4.4 %correlate.9.refs_0_ = f32[16,128]{1,0:T(8,128)S(1)} custom-call(f32[16,128]{1,0:T(8,128)S(1)} %get-tuple-element.37.refs_0_, bf16[16,8,32,384]{3,2,1,0:T(8,128)(2,1)S(1)} %get-tuple-element.38.refs_1_.refs_3_, bf16[8,8,32,384]{3,2,1,0:T(8,128)(2,1)} %refs_2_.1), custom_call_target="tpu_custom_call" | custom-call | flops 1000000 | bytes 1048576 | tf_op jit(solution)/shard_map/correlate/pallas_call | solution.py:214
  31.7 3.5 %collective-permute-done.refs_2_.refs_6_ = bf16[8,3,32,384]{3,2,1,0:T(8,128)(2,1)} collective-permute-done((bf16[8,3,32,384]{3,2,1,0:T(8,128)(2,1)S(1)}, bf16[8,3,32,384]{3,2,1,0:T(8,128)(2,1)}, u32[]{:S(2)}, u32[]{:S(2)}) %collective-permute-start) | collective-permute-done | bytes 589856 | tf_op jit(solution)/shard_map/ppermute | solution.py:563
  38.2 3.1 %correlate.10.refs_0_ = f32[16,128]{1,0:T(8,128)S(1)} custom-call(f32[16,128]{1,0:T(8,128)S(1)} %correlate.9.refs_0_, bf16[16,8,32,384]{3,2,1,0:T(8,128)(2,1)S(1)} %get-tuple-element.38.refs_1_.refs_3_, bf16[8,3,32,384]{3,2,1,0:T(8,128)(2,1)} %collective-permute-done.refs_2_.refs_6_, bf16[8,6,32,384]{3,2,1,0:T(8,128)(2,1)} %collective-permute-done.1.refs_3_.refs_7_), custom_call_target="tpu_custom_call" | custom-call | flops 1000000 | bytes 1048576 | tf_op jit(solution)/shard_map/correlate/pallas_call | solution.py:214
  41.3 3.1 %correlate.11.refs_0_ = f32[16,128]{1,0:T(8,128)S(1)} custom-call(f32[16,128]{1,0:T(8,128)S(1)} %correlate.10.refs_0_, bf16[16,8,32,384]{3,2,1,0:T(8,128)(2,1)S(1)} %get-tuple-element.38.refs_1_.refs_3_, bf16[8,3,32,384]{3,2,1,0:T(8,128)(2,1)} %collective-permute-done.2.refs_2_.refs_6_, bf16[8,6,32,384]{3,2,1,0:T(8,128)(2,1)} %collective-permute-done.1.refs_3_.refs_7_), custom_call_target="tpu_custom_call" | custom-call | flops 1000000 | bytes 1048576 | tf_op jit(solution)/shard_map/correlate/pallas_call | solution.py:214
  44.4 14.7 %collective-permute-done.6.refs_3_.refs_1_.refs_5_.rest_0_.refs_6_ = bf16[24,2,32,384]{3,2,1,0:T(8,128)(2,1)} collective-permute-done((bf16[24,2,32,384]{3,2,1,0:T(8,128)(2,1)}, bf16[24,2,32,384]{3,2,1,0:T(8,128)(2,1)}, u32[]{:S(2)}, u32[]{:S(2)}) %collective-permute-start.6) | collective-permute-done | bytes 1179680 | tf_op jit(solution)/shard_map/ppermute | solution.py:563
  66.7 3.1 %correlate.12.refs_0_ = f32[16,128]{1,0:T(8,128)S(1)} custom-call(f32[16,128]{1,0:T(8,128)S(1)} %correlate.11.refs_0_, bf16[16,8,32,384]{3,2,1,0:T(8,128)(2,1)S(1)} %get-tuple-element.38.refs_1_.refs_3_, bf16[8,6,32,384]{3,2,1,0:T(8,128)(2,1)} %collective-permute-done.3.refs_2_.refs_8_, bf16[8,3,32,384]{3,2,1,0:T(8,128)(2,1)} %collective-permute-done.4.refs_3_.refs_9_), custom_call_target="tpu_custom_call" | custom-call | flops 1000000 | bytes 1048576 | tf_op jit(solution)/shard_map/correlate/pallas_call | solution.py:214
  69.8 3.1 %correlate.13.refs_0_ = f32[16,128]{1,0:T(8,128)S(1)} custom-call(f32[16,128]{1,0:T(8,128)S(1)} %correlate.12.refs_0_, bf16[16,8,32,384]{3,2,1,0:T(8,128)(2,1)S(1)} %get-tuple-element.38.refs_1_.refs_3_, bf16[8,6,32,384]{3,2,1,0:T(8,128)(2,1)} %collective-permute-done.3.refs_2_.refs_8_, bf16[8,3,32,384]{3,2,1,0:T(8,128)(2,1)} %collective-permute-done.5.refs_3_.refs_9_), custom_call_target="tpu_custom_call" | custom-call | flops 1000000 | bytes 1048576 | tf_op jit(solution)/shard_map/correlate/pallas_call | solution.py:214
  73.0 2.7 %correlate.16 = f32[16,128]{1,0:T(8,128)S(1)} custom-call(f32[16,128]{1,0:T(8,128)S(1)} %broadcast_in_dim.74.refs_0_, bf16[24,2,32,384]{3,2,1,0:T(8,128)(2,1)} %collective-permute-done.6.refs_3_.refs_1_.refs_5_.rest_0_.refs_6_, bf16[8,2,32,384]{3,2,1,0:T(8,128)(2,1)S(1)} %slice.15.o_ref.refs_2_.rest_1_.refs_5_, ...), custom_call_target="tpu_custom_call" | custom-call | flops 1000000 | bytes 1048576 | tf_op jit(solution)/shard_map/correlate/pallas_call | solution.py:214
  75.7 2.7 %correlate.14.refs_0_ = f32[16,128]{1,0:T(8,128)S(1)} custom-call(f32[16,128]{1,0:T(8,128)S(1)} %correlate.13.refs_0_, bf16[16,8,32,384]{3,2,1,0:T(8,128)(2,1)S(1)} %get-tuple-element.38.refs_1_.refs_3_, bf16[8,2,32,384]{3,2,1,0:T(8,128)(2,1)S(1)} %slice.15.o_ref.refs_2_.rest_1_.refs_5_, ...), custom_call_target="tpu_custom_call" | custom-call | flops 1000000 | bytes 1048576 | tf_op jit(solution)/shard_map/correlate/pallas_call | solution.py:214
  79.8 7.9 %collective-permute-done.8.refs_2_.refs_10_ = bf16[8,3,32,384]{3,2,1,0:T(8,128)(2,1)S(1)} collective-permute-done((bf16[8,3,32,384]{3,2,1,0:T(8,128)(2,1)}, bf16[8,3,32,384]{3,2,1,0:T(8,128)(2,1)S(1)}, u32[]{:S(2)}, u32[]{:S(2)}) %collective-permute-start.8) | collective-permute-done | bytes 589856 | tf_op jit(solution)/shard_map/ppermute | solution.py:563
  89.0 8.5 %collective-permute-done.9.refs_1_ = f32[16,128]{1,0:T(8,128)S(1)} collective-permute-done((f32[16,128]{1,0:T(8,128)S(1)}, f32[16,128]{1,0:T(8,128)S(1)}, u32[]{:S(2)}, u32[]{:S(2)}) %collective-permute-start.9) | collective-permute-done | bytes 8224 | tf_op jit(solution)/shard_map/ppermute | solution.py:563
  100.1 2.5 %collective-permute-start.14 = (f32[16,128]{1,0:T(8,128)S(1)}, f32[16,128]{1,0:T(8,128)S(1)}, u32[]{:S(2)}, u32[]{:S(2)}) collective-permute-start(f32[16,128]{1,0:T(8,128)S(1)} %add.74), channel_id=1, source_target_pairs={{0,24},{4,28},{8,16},{12,20},{16,8},{20,12},{24,0},{28,4},{1,25},{... | collective-permute-start | bytes 24584 | tf_op jit(solution)/shard_map/ppermute | solution.py:548
  108.2 3.7 %directions.3 = (f32[8,14,32,384]{3,2,1,0:T(8,128)S(1)}, bf16[8,3,32,384]{3,2,1,0:T(8,128)(2,1)S(1)}, bf16[256,512]{1,0:T(8,128)(2,1)S(1)}, f32[3,8,128]{2,1,0:T(8,128)S(1)}) custom-call(f32[16,128]{1,0:T(8,128)S(1)} %add_add_fusion.refs_0_.tot_ref, f32[8,128]{1,0:T(8,128)S(1)} %select_select_fusion.refs_1_.info_ref.refs_0_, ...), custom_call_target="tpu_custom_call" | custom-call | flops 603979776 | bytes 3145728 | tf_op jit(solution)/shard_map/directions/pallas_call | solution.py:373
  111.9 2.1 %removals.1 = f32[8,2,32,384]{3,2,1,0:T(8,128)S(1)} custom-call(f32[8,128]{1,0:T(8,128)S(1)} %select_select_fusion.refs_1_.info_ref.refs_0_, f32[16,128]{1,0:T(8,128)S(1)} %collective-permute-done.15.tot_ref, f32[16,128]{1,0:T(8,128)S(1)} %multiply_add_fusion.refs_2_.cap_ref, ...), custom_call_target="tpu_custom_call" | custom-call | flops 402653184 | bytes 4194304 | tf_op jit(solution)/shard_map/removals/pallas_call | solution.py:412
  116.7 3.4 %directions.4 = (f32[8,14,32,384]{3,2,1,0:T(8,128)S(1)}, bf16[8,3,32,384]{3,2,1,0:T(8,128)(2,1)S(1)}) custom-call(f32[8,128]{1,0:T(8,128)S(1)} %select_select_fusion.refs_1_.info_ref.refs_0_, bf16[256,512]{1,0:T(8,128)(2,1)S(1)} %get-tuple-element.57.refs_1_, f32[3,8,128]{2,1,0:T(8,128)S(1)} %get-tuple-element.58.refs_2_, ...), custom_call_target="tpu_custom_call", output_to_operand_aliasing={{0}: (11, {})} | custom-call | flops 603979776 | bytes 3145728 | tf_op jit(solution)/shard_map/directions/pallas_call | solution.py:373
  120.1 3.2 %collective-permute-start.16 = (bf16[8,3,32,384]{3,2,1,0:T(8,128)(2,1)S(1)}, bf16[8,3,32,384]{3,2,1,0:T(8,128)(2,1)S(1)}, u32[]{:S(2)}, u32[]{:S(2)}) collective-permute-start(bf16[8,3,32,384]{3,2,1,0:T(8,128)(2,1)S(1)} %get-tuple-element.60), channel_id=1, source_target_pairs={{0,4},{4,8},{8,12},{12,16},{16,20},{20,24},{24,28},{1,5},{5,9},{9,... | collective-permute-start | bytes 1769480 | tf_op jit(solution)/shard_map/ppermute | solution.py:657
  125.4 2.7 %directions.5.wide_in = f32[8,14,32,384]{3,2,1,0:T(8,128)S(1)} custom-call(f32[8,128]{1,0:T(8,128)S(1)} %select_select_fusion.refs_1_.info_ref.refs_0_, bf16[256,512]{1,0:T(8,128)(2,1)S(1)} %get-tuple-element.57.refs_1_, f32[3,8,128]{2,1,0:T(8,128)S(1)} %get-tuple-element.58.refs_2_, ...), custom_call_target="tpu_custom_call", output_to_operand_aliasing={{}: (10, {})} | custom-call | flops 402653184 | bytes 67108864 | tf_op jit(solution)/shard_map/directions/pallas_call | solution.py:373
  128.1 7.5 %images.1 = (f32[8,8,32,384]{3,2,1,0:T(8,128)}, f32[8,8,32,384]{3,2,1,0:T(8,128)S(1)}, f32[8,128]{1,0:T(8,128)S(1)}, f32[8,8,32,384]{3,2,1,0:T(8,128)S(1)}, f32[...) custom-call(f32[8,128]{1,0:T(8,128)S(1)} %select_select_fusion.refs_, ...), custom_call_target="tpu_custom_call", output_to_operand_aliasing={{4}: (4, {})} | custom-call | flops 4000000000 | bytes 25165824 | tf_op jit(solution)/shard_map/images/pallas_call | solution.py:476
  135.6 2.1 %collective-permute-start.19 = (f32[8,128]{1,0:T(8,128)S(1)}, f32[8,128]{1,0:T(8,128)S(1)}, u32[]{:S(2)}, u32[]{:S(2)}) collective-permute-start(f32[8,128]{1,0:T(8,128)S(1)} %get-tuple-element.62), channel_id=1, source_target_pairs={{0,4},{4,0},{8,12},{12,8},{16,20},{20,16},{24,28},{28,24},{1,5},{5... | collective-permute-start | bytes 12296 | tf_op jit(solution)/shard_map/ppermute | solution.py:548
  138.5 4.7 %collective-permute-start.22 = (f32[8,128]{1,0:T(8,128)S(1)}, f32[8,128]{1,0:T(8,128)S(1)}, u32[]{:S(2)}, u32[]{:S(2)}) collective-permute-start(f32[8,128]{1,0:T(8,128)S(1)} %add.78), channel_id=1, source_target_pairs={{0,24},{4,28},{8,16},{12,20},{16,8},{20,12},{24,0},{28,4},{1,25},{... | collective-permute-start | bytes 12296 | tf_op jit(solution)/shard_map/ppermute | solution.py:548
  146.8 3.1 %finish.1 = (f32[8,8,32,384]{3,2,1,0:T(8,128)}, f32[8,8,32,384]{3,2,1,0:T(8,128)}) custom-call(f32[16,128]{1,0:T(8,128)S(1)} %add_add_fusion.refs_0_.tot_ref, f32[8,128]{1,0:T(8,128)S(1)} %select_select_fusion.refs_1_.info_ref.refs_0_, f32[8,128]{1,0:T(8,128)S(1)} %add_add_fusion.1.curve_ref, f32[8,8,32,384]{3,2,1,0:T(8,128)S(1)} %get-tuple-element.63.n_ref, ...), custom_call_target="tpu_custom_call" | custom-call | tf_op jit(solution)/shard_map/finish/pallas_call | solution.py:525
  (87 shorter events, 39.8 us)
Async XLA Ops:
  2.2 28.2 %collective-permute-start.1 = (bf16[8,6,32,384]{3,2,1,0:T(8,128)(2,1)S(1)}, bf16[8,6,32,384]{3,2,1,0:T(8,128)(2,1)}, u32[]{:S(2)}, u32[]{:S(2)}) collective-permute-start(bf16[8,6,32,384]{3,2,1,0:T(8,128)(2,1)S(1)} %pad_maximum_fusion), channel_id=1, source_target_pairs={{1,2},{2,1},{5,6},{6,5},{9,10},{10,9},{13,14},{14,13},{17,18},{18,... | collective-permute-start | bytes 3538952 | tf_op jit(solution)/shard_map/ppermute | solution.py:563
  3.9 27.8 %collective-permute-start.2 = (bf16[8,3,32,384]{3,2,1,0:T(8,128)(2,1)S(1)}, bf16[8,3,32,384]{3,2,1,0:T(8,128)(2,1)}, u32[]{:S(2)}, u32[]{:S(2)}) collective-permute-start(bf16[8,3,32,384]{3,2,1,0:T(8,128)(2,1)S(1)} %get-tuple-element.70.refs_5_), channel_id=1, source_target_pairs={{0,1},{1,0},{2,3},{3,2},{4,5},{5,4},{6,7},{7,6},{8,9},{9,8},{10,11... | collective-permute-start | bytes 1769480 | tf_op jit(solution)/shard_map/ppermute | solution.py:563
  8.8 26.4 %collective-permute-start = (bf16[8,3,32,384]{3,2,1,0:T(8,128)(2,1)S(1)}, bf16[8,3,32,384]{3,2,1,0:T(8,128)(2,1)}, u32[]{:S(2)}, u32[]{:S(2)}) collective-permute-start(bf16[8,3,32,384]{3,2,1,0:T(8,128)(2,1)S(1)} %get-tuple-element.71.refs_5_), channel_id=1, source_target_pairs={{0,1},{1,0},{2,3},{3,2},{4,5},{5,4},{6,7},{7,6},{8,9},{9,8},{10,11... | collective-permute-start | bytes 1769480 | tf_op jit(solution)/shard_map/ppermute | solution.py:563
  21.1 38.0 %collective-permute-start.6 = (bf16[24,2,32,384]{3,2,1,0:T(8,128)(2,1)}, bf16[24,2,32,384]{3,2,1,0:T(8,128)(2,1)}, u32[]{:S(2)}, u32[]{:S(2)}) collective-permute-start(bf16[24,2,32,384]{3,2,1,0:T(8,128)(2,1)} %get-tuple-element.42), channel_id=1, source_target_pairs={{0,1},{3,2},{4,5},{7,6},{8,9},{11,10},{12,13},{15,14},{16,17},{19,... | collective-permute-start | bytes 3538952 | tf_op jit(solution)/shard_map/ppermute | solution.py:563
  30.4 31.2 %collective-permute-start.3 = (bf16[8,6,32,384]{3,2,1,0:T(8,128)(2,1)}, bf16[8,6,32,384]{3,2,1,0:T(8,128)(2,1)}, u32[]{:S(2)}, u32[]{:S(2)}) collective-permute-start(bf16[8,6,32,384]{3,2,1,0:T(8,128)(2,1)} %collective-permute-done.1.refs_3_.refs_7_), channel_id=1, source_target_pairs={{1,0},{2,3},{5,4},{6,7},{9,8},{10,11},{13,12},{14,15},{17,16},{18,... | collective-permute-start | bytes 3538952 | tf_op jit(solution)/shard_map/ppermute | solution.py:563
  35.2 9.2 %collective-permute-start.4 = (bf16[8,3,32,384]{3,2,1,0:T(8,128)(2,1)}, bf16[8,3,32,384]{3,2,1,0:T(8,128)(2,1)}, u32[]{:S(2)}, u32[]{:S(2)}) collective-permute-start(bf16[8,3,32,384]{3,2,1,0:T(8,128)(2,1)} %collective-permute-done.refs_2_.refs_6_), channel_id=1, source_target_pairs={{1,2},{2,1},{5,6},{6,5},{9,10},{10,9},{13,14},{14,13},{17,18},{18,... | collective-permute-start | bytes 1769480 | tf_op jit(solution)/shard_map/ppermute | solution.py:563
  36.7 7.7 %collective-permute-start.5 = (bf16[8,3,32,384]{3,2,1,0:T(8,128)(2,1)}, bf16[8,3,32,384]{3,2,1,0:T(8,128)(2,1)}, u32[]{:S(2)}, u32[]{:S(2)}) collective-permute-start(bf16[8,3,32,384]{3,2,1,0:T(8,128)(2,1)} %collective-permute-done.2.refs_2_.refs_6_), channel_id=1, source_target_pairs={{1,2},{2,1},{5,6},{6,5},{9,10},{10,9},{13,14},{14,13},{17,18},{18,... | collective-permute-start | bytes 1769480 | tf_op jit(solution)/shard_map/ppermute | solution.py:563
  61.6 11.4 %collective-permute-start.7 = (bf16[16,2,32,384]{3,2,1,0:T(8,128)(2,1)}, bf16[16,2,32,384]{3,2,1,0:T(8,128)(2,1)}, u32[]{:S(2)}, u32[]{:S(2)}) collective-permute-start(bf16[16,2,32,384]{3,2,1,0:T(8,128)(2,1)} %pad_maximum_fusion.1), channel_id=1, source_target_pairs={{1,2},{2,1},{5,6},{6,5},{9,10},{10,9},{13,14},{14,13},{17,18},{18,... | collective-permute-start | bytes 2359304 | tf_op jit(solution)/shard_map/ppermute | solution.py:563
  63.4 24.4 %collective-permute-start.8 = (bf16[8,3,32,384]{3,2,1,0:T(8,128)(2,1)}, bf16[8,3,32,384]{3,2,1,0:T(8,128)(2,1)S(1)}, u32[]{:S(2)}, u32[]{:S(2)}) collective-permute-start(bf16[8,3,32,384]{3,2,1,0:T(8,128)(2,1)} %collective-permute-done.4.refs_3_.refs_9_), channel_id=1, source_target_pairs={{1,0},{2,3},{5,4},{6,7},{9,8},{10,11},{13,12},{14,15},{17,16},{18,... | collective-permute-start | bytes 1769480 | tf_op jit(solution)/shard_map/ppermute | solution.py:563
  65.4 32.1 %collective-permute-start.10 = (bf16[8,3,32,384]{3,2,1,0:T(8,128)(2,1)}, bf16[8,3,32,384]{3,2,1,0:T(8,128)(2,1)S(1)}, u32[]{:S(2)}, u32[]{:S(2)}) collective-permute-start(bf16[8,3,32,384]{3,2,1,0:T(8,128)(2,1)} %collective-permute-done.5.refs_3_.refs_9_), channel_id=1, source_target_pairs={{1,0},{2,3},{5,4},{6,7},{9,8},{10,11},{13,12},{14,15},{17,16},{18,... | collective-permute-start | bytes 1769480 | tf_op jit(solution)/shard_map/ppermute | solution.py:563
  78.4 19.1 %collective-permute-start.9 = (f32[16,128]{1,0:T(8,128)S(1)}, f32[16,128]{1,0:T(8,128)S(1)}, u32[]{:S(2)}, u32[]{:S(2)}) collective-permute-start(f32[16,128]{1,0:T(8,128)S(1)} %correlate.16), channel_id=1, source_target_pairs={{1,0},{2,3},{5,4},{6,7},{9,8},{10,11},{13,12},{14,15},{17,16},{18,... | collective-permute-start | bytes 24584 | tf_op jit(solution)/shard_map/ppermute | solution.py:563
  79.8 28.4 %copy-start.7 = (bf16[8,3,32,384]{3,2,1,0:T(8,128)(2,1)S(1)}, bf16[8,3,32,384]{3,2,1,0:T(8,128)(2,1)}, u32[]{:S(2)}) copy-start(bf16[8,3,32,384]{3,2,1,0:T(8,128)(2,1)} %copy-done.6) | copy-start | bytes 1769476
  98.9 1.2 collective-permute-start.11
  100.1 4.5 %collective-permute-start.14 = (f32[16,128]{1,0:T(8,128)S(1)}, f32[16,128]{1,0:T(8,128)S(1)}, u32[]{:S(2)}, u32[]{:S(2)}) collective-permute-start(f32[16,128]{1,0:T(8,128)S(1)} %add.74), channel_id=1, source_target_pairs={{0,24},{4,28},{8,16},{12,20},{16,8},{20,12},{24,0},{28,4},{1,25},{... | collective-permute-start | bytes 24584 | tf_op jit(solution)/shard_map/ppermute | solution.py:548
  102.5 3.7 %collective-permute-start.13 = (f32[16,128]{1,0:T(8,128)S(1)}, f32[16,128]{1,0:T(8,128)S(1)}, u32[]{:S(2)}, u32[]{:S(2)}) collective-permute-start(f32[16,128]{1,0:T(8,128)S(1)} %add.74), channel_id=1, source_target_pairs={{0,16},{4,20},{8,24},{12,28},{16,0},{20,4},{24,8},{28,12},{1,17},{... | collective-permute-start | bytes 24584 | tf_op jit(solution)/shard_map/ppermute | solution.py:548
  103.0 3.7 %collective-permute-start.12 = (f32[16,128]{1,0:T(8,128)S(1)}, f32[16,128]{1,0:T(8,128)S(1)}, u32[]{:S(2)}, u32[]{:S(2)}) collective-permute-start(f32[16,128]{1,0:T(8,128)S(1)} %add.74), channel_id=1, source_target_pairs={{0,8},{4,12},{8,0},{12,4},{16,24},{20,28},{24,16},{28,20},{1,9},{5... | collective-permute-start | bytes 24584 | tf_op jit(solution)/shard_map/ppermute | solution.py:548
  106.7 5.2 %collective-permute-start.15 = (f32[16,128]{1,0:T(8,128)S(1)}, f32[16,128]{1,0:T(8,128)S(1)}, u32[]{:S(2)}, u32[]{:S(2)}) collective-permute-start(f32[16,128]{1,0:T(8,128)S(1)} %add_add_fusion.refs_0_.tot_ref), channel_id=1, source_target_pairs={{0,1},{3,2},{4,5},{7,6},{8,9},{11,10},{12,13},{15,14},{16,17},{19,... | collective-permute-start | bytes 24584 | tf_op jit(solution)/shard_map/ppermute | solution.py:563
  114.1 11.2 %collective-permute-start.18 = (f16[8,2,32,384]{3,2,1,0:T(8,128)(2,1)S(1)}, f16[8,2,32,384]{3,2,1,0:T(8,128)(2,1)S(1)}, u32[]{:S(2)}, u32[]{:S(2)}) collective-permute-start(f16[8,2,32,384]{3,2,1,0:T(8,128)(2,1)S(1)} %multiply_convert_fusion), channel_id=1, source_target_pairs={{1,0},{2,3},{5,4},{6,7},{9,8},{10,11},{13,12},{14,15},{17,16},{18,... | collective-permute-start | bytes 1179656 | tf_op jit(solution)/shard_map/ppermute | solution.py:563
  115.4 12.7 %collective-permute-start.17 = (bf16[8,3,32,384]{3,2,1,0:T(8,128)(2,1)S(1)}, bf16[8,3,32,384]{3,2,1,0:T(8,128)(2,1)S(1)}, u32[]{:S(2)}, u32[]{:S(2)}) collective-permute-start(bf16[8,3,32,384]{3,2,1,0:T(8,128)(2,1)S(1)} %get-tuple-element.54), channel_id=1, source_target_pairs={{4,0},{8,4},{12,8},{16,12},{20,16},{24,20},{28,24},{5,1},{9,5},{13... | collective-permute-start | bytes 1769480 | tf_op jit(solution)/shard_map/ppermute | solution.py:653
  120.1 8.0 %collective-permute-start.16 = (bf16[8,3,32,384]{3,2,1,0:T(8,128)(2,1)S(1)}, bf16[8,3,32,384]{3,2,1,0:T(8,128)(2,1)S(1)}, u32[]{:S(2)}, u32[]{:S(2)}) collective-permute-start(bf16[8,3,32,384]{3,2,1,0:T(8,128)(2,1)S(1)} %get-tuple-element.60), channel_id=1, source_target_pairs={{0,4},{4,8},{8,12},{12,16},{16,20},{20,24},{24,28},{1,5},{5,9},{9,... | collective-permute-start | bytes 1769480 | tf_op jit(solution)/shard_map/ppermute | solution.py:657
  135.6 2.9 %collective-permute-start.19 = (f32[8,128]{1,0:T(8,128)S(1)}, f32[8,128]{1,0:T(8,128)S(1)}, u32[]{:S(2)}, u32[]{:S(2)}) collective-permute-start(f32[8,128]{1,0:T(8,128)S(1)} %get-tuple-element.62), channel_id=1, source_target_pairs={{0,4},{4,0},{8,12},{12,8},{16,20},{20,16},{24,28},{28,24},{1,5},{5... | collective-permute-start | bytes 12296 | tf_op jit(solution)/shard_map/ppermute | solution.py:548
  138.5 6.7 %collective-permute-start.22 = (f32[8,128]{1,0:T(8,128)S(1)}, f32[8,128]{1,0:T(8,128)S(1)}, u32[]{:S(2)}, u32[]{:S(2)}) collective-permute-start(f32[8,128]{1,0:T(8,128)S(1)} %add.78), channel_id=1, source_target_pairs={{0,24},{4,28},{8,16},{12,20},{16,8},{20,12},{24,0},{28,4},{1,25},{... | collective-permute-start | bytes 12296 | tf_op jit(solution)/shard_map/ppermute | solution.py:548
  143.2 3.6 %collective-permute-start.21 = (f32[8,128]{1,0:T(8,128)S(1)}, f32[8,128]{1,0:T(8,128)S(1)}, u32[]{:S(2)}, u32[]{:S(2)}) collective-permute-start(f32[8,128]{1,0:T(8,128)S(1)} %add.78), channel_id=1, source_target_pairs={{0,16},{4,20},{8,24},{12,28},{16,0},{20,4},{24,8},{28,12},{1,17},{... | collective-permute-start | bytes 12296 | tf_op jit(solution)/shard_map/ppermute | solution.py:548
  143.2 3.6 %collective-permute-start.20 = (f32[8,128]{1,0:T(8,128)S(1)}, f32[8,128]{1,0:T(8,128)S(1)}, u32[]{:S(2)}, u32[]{:S(2)}) collective-permute-start(f32[8,128]{1,0:T(8,128)S(1)} %add.78), channel_id=1, source_target_pairs={{0,8},{4,12},{8,0},{12,4},{16,24},{20,28},{24,16},{28,20},{1,9},{5... | collective-permute-start | bytes 12296 | tf_op jit(solution)/shard_map/ppermute | solution.py:548
  (11 other events, 117.9 us)
